TPU v7x, 32 devices: a whole 2x2x4 slice. The times are simulated.
32 devices in a mesh: seq: 4 (over y, core), items: 8 (over z, x).
Axes of the slice: x: 2, y: 2, z: 4, core: 2. Of those that a mesh axis runs over, the one named last changes fastest.
Arguments:
- block_in: bfloat16 [16, 640, 768], P('items', 'seq'), may hold values from -6 to 6
- lengths: int32 [16], P('items'), may hold values from 257 to 577, as said below
- gain_attn: float32 [768], replicated, may hold values from 0.5 to 1.5
- w_query: bfloat16 [768, 768], replicated, may hold values from -0.21875 to 0.21875
- w_key: bfloat16 [768, 768], replicated, may hold values from -0.21875 to 0.21875
- w_value: bfloat16 [768, 768], replicated, may hold values from -0.21875 to 0.21875
- w_out: bfloat16 [768, 768], replicated, may hold values from -1.75 to 1.75
- gain_ffn: float32 [768], replicated, may hold values from 0.5 to 1.5
- w_gate: bfloat16 [768, 2048], replicated, may hold values from -0.21875 to 0.21875
- w_up: bfloat16 [768, 2048], replicated, may hold values from -0.21875 to 0.21875
- w_down: bfloat16 [2048, 768], replicated, may hold values from -0.125 to 0.125
- cotangent: bfloat16 [16, 640, 768], P('items', 'seq'), may hold values from -6 to 6
Outputs:
- block_out: bfloat16 [16, 640, 768], P('items', 'seq')
- grad_input: bfloat16 [16, 640, 768], P('items', 'seq')
- grad_gain_attn: float32 [768], P('items')
- grad_w_query: float32 [768, 768], P('items')
- grad_w_key: float32 [768, 768], P('items')
- grad_w_value: float32 [768, 768], P('items')
- grad_w_out: float32 [768, 768], P('items')
- grad_gain_ffn: float32 [768], P('items')
- grad_w_gate: float32 [768, 2048], P('items')
- grad_w_up: float32 [768, 2048], P('items')
- grad_w_down: float32 [2048, 768], P('items')
Inputs may be any that keep to these rules, and one draw needn't show every extreme that they name: `lengths`: each item's length is 257 or 577; in each aligned block of 2 items at least one has 577.
All inputs are finite; a program needn't handle non-finite values.
Results may differ from a plain program's by a relative error of at most 0.02.
Values may be sent and summed in bfloat16 or wider, within the bound.
A program may use at most 128 MiB of HBM per device.

v0:
```python
import jax
import jax.numpy as jnp
from jax import lax
from jax.sharding import PartitionSpec as P

HD = 64
SIDE_S = 16
SIDE_L = 24
LONG = 577


epsilon = 1e-05


def grid_places(lengths, rows):
    side = jnp.where(lengths == LONG, SIDE_L, SIDE_S).astype(jnp.int32)[:, None]
    place = rows[None, :] - 1
    valid = (place >= 0) & (rows[None, :] < lengths[:, None])
    place = jnp.where(valid, place, 0)
    return (place // side, place % side)


def rotary_tables(lengths, rows):
    grid_row, grid_col = grid_places(lengths, rows)
    quarter = HD // 4
    freq = 10000.0 ** (-jnp.arange(quarter, dtype=jnp.float32) / quarter)
    angle_row = grid_row[..., None].astype(jnp.float32) * freq
    angle_col = grid_col[..., None].astype(jnp.float32) * freq
    cosine = jnp.concatenate(
        [jnp.cos(angle_row), jnp.cos(angle_row), jnp.cos(angle_col), jnp.cos(angle_col)], -1
    )
    sine = jnp.concatenate(
        [jnp.sin(angle_row), jnp.sin(angle_row), jnp.sin(angle_col), jnp.sin(angle_col)], -1
    )
    return (cosine[:, :, None, :], sine[:, :, None, :])


def turn(values):
    quarter = HD // 4
    first = values[..., 0:quarter]
    second = values[..., quarter : 2 * quarter]
    third = values[..., 2 * quarter : 3 * quarter]
    fourth = values[..., 3 * quarter :]
    return jnp.concatenate([-second, first, -fourth, third], -1)


def project(left, right):
    return jnp.einsum("ird,de->ire", left, right, preferred_element_type=jnp.float32)


def back_project(grad, weight):
    return jnp.einsum("ire,de->ird", grad, weight, preferred_element_type=jnp.float32)


def weight_grad(left, right):
    return jnp.einsum("ird,ire->de", left, right, preferred_element_type=jnp.float32)


def norm_back(grad_normed, unit, scale, gain):
    scaled = grad_normed * gain
    return scale * (scaled - unit * jnp.mean(scaled * unit, -1, keepdims=True))


def body(
    block_in,
    lengths,
    gain_attn,
    w_query,
    w_key,
    w_value,
    w_out,
    gain_ffn,
    w_gate,
    w_up,
    w_down,
    cotangent,
):
    count, rows_here, width = block_in.shape
    heads = width // HD
    length_all = rows_here * lax.axis_size("seq")
    factor = HD ** (-0.5)
    query_rows = lax.axis_index("seq") * rows_here + jnp.arange(rows_here, dtype=jnp.int32)
    key_rows = jnp.arange(length_all, dtype=jnp.int32)
    cosine, sine = rotary_tables(lengths, query_rows)
    allowed = (key_rows[None, None, :] <= query_rows[None, :, None]) & (
        key_rows[None, None, :] < lengths[:, None, None]
    )

    def heads_of(array):
        return array.reshape(array.shape[0], array.shape[1], heads, HD)

    def attention_scores(query, keys_all):
        raw = (
            jnp.einsum(
                "irhe,iphe->ihrp", query, heads_of(keys_all), preferred_element_type=jnp.float32
            )
            * factor
        )
        return jnp.where(allowed[:, None], raw, -1e30)

    source = block_in.astype(jnp.float32)
    scale_attn = lax.rsqrt(jnp.mean(source * source, -1, keepdims=True) + epsilon)
    unit_attn = source * scale_attn
    normed = (unit_attn * gain_attn).astype(jnp.bfloat16)
    query_pre = heads_of(project(normed, w_query))
    keys_pre = heads_of(project(normed, w_key))
    query = (query_pre * cosine + turn(query_pre) * sine).astype(jnp.bfloat16)
    keys = (
        (keys_pre * cosine + turn(keys_pre) * sine)
        .astype(jnp.bfloat16)
        .reshape(count, rows_here, width)
    )
    values = project(normed, w_value).astype(jnp.bfloat16)
    keys_all, values_all = (
        lax.all_gather(keys, "seq", axis=1, tiled=True),
        lax.all_gather(values, "seq", axis=1, tiled=True),
    )
    scores = attention_scores(query, keys_all)
    top = jnp.max(scores, -1, keepdims=True)
    expo = jnp.exp(scores - top)
    summed = jnp.sum(expo, -1, keepdims=True)
    chance = expo / summed
    log_total = top + jnp.log(summed)
    mixed = (
        jnp.einsum(
            "ihrp,iphe->irhe",
            chance.astype(jnp.bfloat16),
            heads_of(values_all),
            preferred_element_type=jnp.float32,
        )
        .reshape(count, rows_here, width)
        .astype(jnp.bfloat16)
    )
    middle = source + project(mixed, w_out)
    scale_ffn = lax.rsqrt(jnp.mean(middle * middle, -1, keepdims=True) + epsilon)
    unit_ffn = middle * scale_ffn
    normed_ffn = (unit_ffn * gain_ffn).astype(jnp.bfloat16)
    gate = project(normed_ffn, w_gate)
    up = project(normed_ffn, w_up)
    sigma = jax.nn.sigmoid(gate)
    hidden = (gate * sigma * up).astype(jnp.bfloat16)
    block_out = (middle + project(hidden, w_down)).astype(jnp.bfloat16)
    incoming = cotangent.astype(jnp.float32)
    grad_w_down = weight_grad(hidden, cotangent)
    grad_hidden = back_project(cotangent, w_down)
    grad_gate = (grad_hidden * up * sigma * (1.0 + gate * (1.0 - sigma))).astype(jnp.bfloat16)
    grad_up = (grad_hidden * gate * sigma).astype(jnp.bfloat16)
    grad_w_gate = weight_grad(normed_ffn, grad_gate)
    grad_w_up = weight_grad(normed_ffn, grad_up)
    grad_normed_ffn = back_project(grad_gate, w_gate) + back_project(grad_up, w_up)
    grad_gain_ffn = jnp.sum(grad_normed_ffn * unit_ffn, axis=(0, 1))
    grad_middle = incoming + norm_back(grad_normed_ffn, unit_ffn, scale_ffn, gain_ffn)
    grad_branch = grad_middle.astype(jnp.bfloat16)
    grad_w_out = weight_grad(mixed, grad_branch)
    grad_mixed = heads_of(back_project(grad_branch, w_out)).astype(jnp.bfloat16)
    keys_back, values_back = (keys_all, values_all)
    chance_back = jnp.exp(attention_scores(query, keys_back) - log_total)
    grad_chance = jnp.einsum(
        "irhe,iphe->ihrp", grad_mixed, heads_of(values_back), preferred_element_type=jnp.float32
    )
    inner = jnp.sum(grad_chance * chance_back, -1, keepdims=True)
    grad_scores = (chance_back * (grad_chance - inner)).astype(jnp.bfloat16)
    grad_query = (
        jnp.einsum(
            "ihrp,iphe->irhe", grad_scores, heads_of(keys_back), preferred_element_type=jnp.float32
        )
        * factor
    )
    grad_values_sum = jnp.einsum(
        "ihrp,irhe->iphe",
        chance_back.astype(jnp.bfloat16),
        grad_mixed,
        preferred_element_type=jnp.float32,
    )
    grad_keys_sum = (
        jnp.einsum("ihrp,irhe->iphe", grad_scores, query, preferred_element_type=jnp.float32)
        * factor
    )
    grad_keys, grad_values = (
        lax.psum_scatter(
            grad_keys_sum.reshape(count, length_all, width).astype(jnp.bfloat16),
            "seq",
            scatter_dimension=1,
            tiled=True,
        ).astype(jnp.float32),
        lax.psum_scatter(
            grad_values_sum.reshape(count, length_all, width).astype(jnp.bfloat16),
            "seq",
            scatter_dimension=1,
            tiled=True,
        ).astype(jnp.float32),
    )
    grad_query_pre = (
        (grad_query * cosine - turn(grad_query * sine))
        .reshape(count, rows_here, width)
        .astype(jnp.bfloat16)
    )
    grad_keys_heads = heads_of(grad_keys)
    grad_keys_pre = (
        (grad_keys_heads * cosine - turn(grad_keys_heads * sine))
        .reshape(count, rows_here, width)
        .astype(jnp.bfloat16)
    )
    grad_values_pre = grad_values.astype(jnp.bfloat16)
    grad_w_query = weight_grad(normed, grad_query_pre)
    grad_w_key = weight_grad(normed, grad_keys_pre)
    grad_w_value = weight_grad(normed, grad_values_pre)
    grad_normed = (
        back_project(grad_query_pre, w_query)
        + back_project(grad_keys_pre, w_key)
        + back_project(grad_values_pre, w_value)
    )
    grad_gain_attn = jnp.sum(grad_normed * unit_attn, axis=(0, 1))
    grad_input = (grad_middle + norm_back(grad_normed, unit_attn, scale_attn, gain_attn)).astype(
        jnp.bfloat16
    )
    shares = (
        lax.psum_scatter(
            grad_gain_attn.astype(jnp.bfloat16), "items", scatter_dimension=0, tiled=True
        ).astype(jnp.float32),
        lax.psum_scatter(
            grad_w_query.astype(jnp.bfloat16), "items", scatter_dimension=0, tiled=True
        ).astype(jnp.float32),
        lax.psum_scatter(
            grad_w_key.astype(jnp.bfloat16), "items", scatter_dimension=0, tiled=True
        ).astype(jnp.float32),
        lax.psum_scatter(
            grad_w_value.astype(jnp.bfloat16), "items", scatter_dimension=0, tiled=True
        ).astype(jnp.float32),
        lax.psum_scatter(
            grad_w_out.astype(jnp.bfloat16), "items", scatter_dimension=0, tiled=True
        ).astype(jnp.float32),
        lax.psum_scatter(
            grad_gain_ffn.astype(jnp.bfloat16), "items", scatter_dimension=0, tiled=True
        ).astype(jnp.float32),
        lax.psum_scatter(
            grad_w_gate.astype(jnp.bfloat16), "items", scatter_dimension=0, tiled=True
        ).astype(jnp.float32),
        lax.psum_scatter(
            grad_w_up.astype(jnp.bfloat16), "items", scatter_dimension=0, tiled=True
        ).astype(jnp.float32),
        lax.psum_scatter(
            grad_w_down.astype(jnp.bfloat16), "items", scatter_dimension=0, tiled=True
        ).astype(jnp.float32),
    )
    summed = (
        lax.psum(shares[0].astype(jnp.bfloat16), "seq").astype(jnp.float32),
        lax.psum(shares[1].astype(jnp.bfloat16), "seq").astype(jnp.float32),
        lax.psum(shares[2].astype(jnp.bfloat16), "seq").astype(jnp.float32),
        lax.psum(shares[3].astype(jnp.bfloat16), "seq").astype(jnp.float32),
        lax.psum(shares[4].astype(jnp.bfloat16), "seq").astype(jnp.float32),
        lax.psum(shares[5].astype(jnp.bfloat16), "seq").astype(jnp.float32),
        lax.psum(shares[6].astype(jnp.bfloat16), "seq").astype(jnp.float32),
        lax.psum(shares[7].astype(jnp.bfloat16), "seq").astype(jnp.float32),
        lax.psum(shares[8].astype(jnp.bfloat16), "seq").astype(jnp.float32),
    )
    return (
        block_out,
        grad_input,
        summed[0],
        summed[1],
        summed[2],
        summed[3],
        summed[4],
        summed[5],
        summed[6],
        summed[7],
        summed[8],
    )


def solution(mesh):
    return jax.shard_map(
        body,
        mesh=mesh,
        in_specs=(
            P("items", "seq", None),
            P("items"),
            P(),
            P(),
            P(),
            P(),
            P(),
            P(),
            P(),
            P(),
            P(),
            P("items", "seq", None),
        ),
        out_specs=(
            P("items", "seq", None),
            P("items", "seq", None),
            P("items"),
            P("items", None),
            P("items", None),
            P("items", None),
            P("items", None),
            P("items"),
            P("items", None),
            P("items", None),
            P("items", None),
        ),
        check_vma=False,
    )
```

profile of v0, /device:TPU:1, one launch (start us, length us, event | category | flops | bytes accessed | tf_op | source)
XLA Modules:
  0.0 771.6 jit_solution(6032717731386892933)
XLA Ops:
  9.4 3.0 fusion.42
  35.7 4.8 fusion.6
  40.5 15.8 %all-gather.5.cloned.1.call-done = bf16[2,640,768]{2,1,0:T(8,128)(2,1)} async-done(((bf16[2,160,768]{2,1,0:T(8,128)(2,1)}), bf16[2,640,768]{2,1,0:T(8,128)(2,1)}) %all-gather.5.cloned.1.call-update) | async-done | bytes 1966096 | tf_op jit(solution)/shard_map/all_gather | solution.py:115
  56.3 4.0 copy.67
  60.3 3.8 fusion.69
  67.9 12.4 %all-gather.3.cloned.1.call-done = bf16[2,640,768]{2,1,0:T(8,128)(2,1)} async-done(((bf16[2,160,768]{2,1,0:T(8,128)(2,1)}), bf16[2,640,768]{2,1,0:T(8,128)(2,1)}) %all-gather.3.cloned.1.call-update) | async-done | bytes 1966096 | tf_op jit(solution)/shard_map/all_gather | solution.py:116
  80.3 4.1 copy.62
  84.5 7.2 fusion.29
  96.2 3.2 multiply_convert_fusion.3
  106.3 7.5 multiply_reduce_fusion
  118.4 4.5 copy.71
  123.0 5.8 fusion.18
  131.3 3.1 bitcast_convert_fusion.3
  134.5 4.5 bitcast_multiply_fusion
  144.2 27.7 %all-reduce.9.cloned.1.call-done = bf16[2,640,768]{2,0,1:T(2,128)(2,1)} async-done(((bf16[2,640,768]{2,0,1:T(2,128)(2,1)}), bf16[2,640,768]{2,0,1:T(2,128)(2,1)}) %all-reduce.9.cloned.1.call-update) | async-done | bytes 1966096
  177.5 4.8 bitcast_convert_fusion.2
  182.6 4.9 bitcast_convert_fusion.1
  188.5 4.9 bitcast_convert_fusion
  193.5 11.6 %reduce-scatter.9.cloned.1.call-done = bf16[2,160,768]{2,1,0:T(8,128)(2,1)} async-done(((bf16[2,640,768]{2,1,0:T(8,128)(2,1)}), bf16[2,160,768]{2,1,0:T(8,128)(2,1)}) %reduce-scatter.9.cloned.1.call-update) | async-done | bytes 491536 | tf_op jit(solution)/shard_map/reduce_scatter | solution.py:186
  205.1 3.1 bitcast_convert_fusion.4
  209.5 3.4 fusion.44
  212.9 3.9 fusion.36
  216.7 54.5 %reduce-scatter.17.cloned.1.call-done = bf16[96,768]{1,0:T(8,128)(2,1)} async-done(((bf16[768,768]{1,0:T(8,128)(2,1)}), bf16[96,768]{1,0:T(8,128)(2,1)}) %reduce-scatter.17.cloned.1.call-update) | async-done | bytes 147472 | tf_op jit(solution)/shard_map/reduce_scatter | solution.py:230
  271.2 66.8 %reduce-scatter.11.cloned.1.call-done = bf16[96,768]{1,0:T(8,128)(2,1)} async-done(((bf16[768,768]{1,0:T(8,128)(2,1)}), bf16[96,768]{1,0:T(8,128)(2,1)}) %reduce-scatter.11.cloned.1.call-update) | async-done | bytes 147472 | tf_op jit(solution)/shard_map/reduce_scatter | solution.py:221
  338.0 67.0 %reduce-scatter.13.cloned.1.call-done = bf16[96,768]{1,0:T(8,128)(2,1)} async-done(((bf16[768,768]{1,0:T(8,128)(2,1)}), bf16[96,768]{1,0:T(8,128)(2,1)}) %reduce-scatter.13.cloned.1.call-update) | async-done | bytes 147472 | tf_op jit(solution)/shard_map/reduce_scatter | solution.py:224
  405.0 78.3 %reduce-scatter.19.cloned.1.call-done = bf16[96,2048]{1,0:T(8,128)(2,1)} async-done(((bf16[768,2048]{1,0:T(8,128)(2,1)}), bf16[96,2048]{1,0:T(8,128)(2,1)}) %reduce-scatter.19.cloned.1.call-update) | async-done | bytes 393232 | tf_op jit(solution)/shard_map/reduce_scatter | solution.py:236
  483.3 77.4 %reduce-scatter.21.cloned.1.call-done = bf16[96,2048]{1,0:T(8,128)(2,1)} async-done(((bf16[768,2048]{1,0:T(8,128)(2,1)}), bf16[96,2048]{1,0:T(8,128)(2,1)}) %reduce-scatter.21.cloned.1.call-update) | async-done | bytes 393232 | tf_op jit(solution)/shard_map/reduce_scatter | solution.py:239
  560.7 77.2 %reduce-scatter.23.cloned.1.call-done = bf16[256,768]{1,0:T(8,128)(2,1)} async-done(((bf16[2048,768]{1,0:T(8,128)(2,1)}), bf16[256,768]{1,0:T(8,128)(2,1)}) %reduce-scatter.23.cloned.1.call-update) | async-done | bytes 393232 | tf_op jit(solution)/shard_map/reduce_scatter | solution.py:242
  638.0 66.2 %reduce-scatter.15.cloned.1.call-done = bf16[96,768]{1,0:T(8,128)(2,1)} async-done(((bf16[768,768]{1,0:T(8,128)(2,1)}), bf16[96,768]{1,0:T(8,128)(2,1)}) %reduce-scatter.15.cloned.1.call-update) | async-done | bytes 147472 | tf_op jit(solution)/shard_map/reduce_scatter | solution.py:227
  707.5 15.7 %all-reduce.3 = (bf16[768]{0:T(1024)(128)(2,1)S(1)}, bf16[768]{0:T(1024)(128)(2,1)S(1)}) all-reduce(bf16[768]{0:T(1024)(128)(2,1)S(1)} %get-tuple-element.13, bf16[768]{0:T(1024)(128)(2,1)S(1)} %get-tuple-element.11), channel_id=4, replica_groups=mesh['seq'=4,'items'=8] {'items'}, use_global_device_ids=true, to_apply=%region_10.11.clone | all-reduce | flops 1536 | bytes 6144
  723.3 11.0 %all-reduce.4 = (bf16[96]{0:T(256)(128)(2,1)S(1)}, bf16[96]{0:T(256)(128)(2,1)S(1)}) all-reduce(bf16[96]{0:T(256)(128)(2,1)S(1)} %dynamic-slice.3, bf16[96]{0:T(256)(128)(2,1)S(1)} %dynamic-slice.5), channel_id=1, replica_groups=mesh['seq'=4,'items'=8] {'seq'}, use_global_device_ids=true, to_apply=%region_11.12 | all-reduce | flops 192 | bytes 768 | tf_op jit(solution)/shard_map/psum | solution.py:247
  736.4 18.2 %all-reduce.11.cloned.1.call-done = (bf16[96,768]{1,0:T(8,128)(2,1)}, bf16[96,768]{1,0:T(8,128)(2,1)}, bf16[96,768]{1,0:T(8,128)(2,1)}, bf16[96,768]{1,0:T(8,128...) async-done(((bf16[96,768]{1,0:T(8,128)(2,1)}, bf16[96,768]{1,0:T(8,128)(2,1)}, bf16[96,768]{1,0:T(8,128)(2,1)}, ...) | async-done | bytes 1769488 | tf_op jit(solution)/shard_map/psum | solution.py:248
  (171 shorter events, 74.7 us)
Async XLA Ops:
  7.2 88.3 %copy-start = (bf16[768,2048]{1,0:T(8,128)(2,1)S(1)}, bf16[768,2048]{1,0:T(8,128)(2,1)}, u32[]{:S(2)}) copy-start(bf16[768,2048]{1,0:T(8,128)(2,1)} %param.20) | copy-start | bytes 9437188
  7.2 49.1 %all-gather.5.cloned.1.call-start = ((), (), s32[]{:S(2)}) async-start(), calls=%async_computation.9 | async-start | bytes 2457600 | tf_op jit(solution)/shard_map/all_gather | solution.py:115
  9.4 5.9 copy-start.31
  16.5 4.2 copy-start.29
  31.8 48.5 %all-gather.3.cloned.1.call-start = ((), (), s32[]{:S(2)}) async-start(), calls=%async_computation.8 | async-start | bytes 2457600 | tf_op jit(solution)/shard_map/all_gather | solution.py:116
  34.7 137.2 %all-reduce.9.cloned.1.call-start = ((), (), s32[]{:S(2)}) async-start(), calls=%async_computation.18 | async-start | bytes 3932160
  64.1 3.8 copy-start.2
  84.5 7.3 copy-start.5
  84.5 7.3 copy-start.22
  92.5 9.9 %copy-start.11 = (f32[2,160,768]{2,1,0:T(8,128)}, f32[2,160,768]{2,1,0:T(8,128)S(1)}, u32[]{:S(2)}) copy-start(f32[2,160,768]{2,1,0:T(8,128)S(1)} %get-tuple-element.65) | copy-start | bytes 2949124
  102.8 3.6 copy-start.7
  106.3 7.6 slice-start
  106.3 7.6 slice-start.1
  106.3 7.6 slice-start.2
  122.9 82.1 %reduce-scatter.9.cloned.1.call-start = ((), (), s32[]{:S(2)}) async-start(), calls=%async_computation.10 | async-start | bytes 2457600 | tf_op jit(solution)/shard_map/reduce_scatter | solution.py:186
  131.2 3.3 copy-start.4
  131.2 140.0 %reduce-scatter.17.cloned.1.call-start = ((), (), s32[]{:S(2)}) async-start(), calls=%async_computation.14 | async-start | bytes 1327104 | tf_op jit(solution)/shard_map/reduce_scatter | solution.py:230
  134.4 203.6 %reduce-scatter.11.cloned.1.call-start = ((), (), s32[]{:S(2)}) async-start(), calls=%async_computation.11 | async-start | bytes 1327104 | tf_op jit(solution)/shard_map/reduce_scatter | solution.py:221
  142.9 262.1 %reduce-scatter.13.cloned.1.call-start = ((), (), s32[]{:S(2)}) async-start(), calls=%async_computation.12 | async-start | bytes 1327104 | tf_op jit(solution)/shard_map/reduce_scatter | solution.py:224
  177.5 305.8 %reduce-scatter.19.cloned.1.call-start = ((), (), s32[]{:S(2)}) async-start(), calls=%async_computation.15 | async-start | bytes 3538944 | tf_op jit(solution)/shard_map/reduce_scatter | solution.py:236
  182.3 378.4 %reduce-scatter.21.cloned.1.call-start = ((), (), s32[]{:S(2)}) async-start(), calls=%async_computation.16 | async-start | bytes 3538944 | tf_op jit(solution)/shard_map/reduce_scatter | solution.py:239
  187.5 450.4 %reduce-scatter.23.cloned.1.call-start = ((), (), s32[]{:S(2)}) async-start(), calls=%async_computation.17 | async-start | bytes 3538944 | tf_op jit(solution)/shard_map/reduce_scatter | solution.py:242
  193.4 14.8 %copy-start.33 = (u32[32]{0:T(128)S(1)}, u32[32]{0:T(128)}, u32[]{:S(2)}) copy-start(u32[32]{0:T(128)} %constant.66) | copy-start | bytes 388
  193.4 510.8 %reduce-scatter.15.cloned.1.call-start = ((), (), s32[]{:S(2)}) async-start(), calls=%async_computation.13 | async-start | bytes 1327104 | tf_op jit(solution)/shard_map/reduce_scatter | solution.py:227
  208.1 4.8 copy-start.12
  208.2 546.5 %all-reduce.11.cloned.1.call-start = ((), (), s32[]{:S(2)}) async-start(), calls=%async_computation.19 | async-start | bytes 3538944 | tf_op jit(solution)/shard_map/psum | solution.py:248
  209.5 3.4 copy-start.36
  216.7 487.5 %copy-start.10 = (bf16[768,768]{1,0:T(8,128)(2,1)S(1)}, bf16[768,768]{1,0:T(8,128)(2,1)}, u32[]{:S(2)}) copy-start(bf16[768,768]{1,0:T(8,128)(2,1)} %param.16) | copy-start | bytes 3538948
  754.7 6.8 copy-start.28
  754.7 7.8 %copy-start.27 = (bf16[96,2048]{1,0:T(8,128)(2,1)S(1)}, bf16[96,2048]{1,0:T(8,128)(2,1)}, u32[]{:S(2)}) copy-start(bf16[96,2048]{1,0:T(8,128)(2,1)} %get-tuple-element.24) | copy-start | bytes 1179652
  754.7 8.7 %copy-start.26 = (bf16[256,768]{1,0:T(8,128)(2,1)S(1)}, bf16[256,768]{1,0:T(8,128)(2,1)}, u32[]{:S(2)}) copy-start(bf16[256,768]{1,0:T(8,128)(2,1)} %get-tuple-element.25) | copy-start | bytes 1179652
  759.7 4.6 copy-start.1
  (21 other events, 37.8 us)
Sparse Core Ops, SparseCore 0:
  31.9 24.3 all-gather.4
  58.4 21.8 all-gather.2
  123.1 48.7 all-reduce.8
  174.3 30.7 reduce-scatter.8
  208.7 62.5 reduce-scatter.16
  274.9 63.0 reduce-scatter.10
  341.8 63.1 reduce-scatter.12
  409.0 74.2 reduce-scatter.18
  487.3 73.3 reduce-scatter.20
  564.6 73.3 reduce-scatter.22
  641.7 62.4 reduce-scatter.14
  707.2 47.4 all-reduce.10
where the time goes:
time: 781 us; the launch traced here: 772 us
  waiting for transfers between devices  573 us (73%)
  matrix products  87 us (11%)
  local copies, waits for them, and re-layouts  39.3 us (5%)
  other arithmetic  28 us (4%)
  blocking collectives  26.7 us (3%)
  between operations  16.6 us (2%)
    reduce_scatter x1, waiting for transfers between devices, body(): lax.psum_scatter(grad_w_gate.astype(jnp.bfloat16), 'items', scatter_dimen...  78.3 us
    reduce_scatter x1, waiting for transfers between devices, body(): lax.psum_scatter(grad_w_up.astype(jnp.bfloat16), 'items', scatter_dimensi...  77.4 us
    reduce_scatter x1, waiting for transfers between devices, body(): lax.psum_scatter(grad_w_down.astype(jnp.bfloat16), 'items', scatter_dimen...  77.2 us
    reduce_scatter x1, waiting for transfers between devices, body(): lax.psum_scatter(grad_w_key.astype(jnp.bfloat16), 'items', scatter_dimens...  67 us
    reduce_scatter x1, waiting for transfers between devices, body(): lax.psum_scatter(grad_w_query.astype(jnp.bfloat16), 'items', scatter_dime...  66.8 us
    reduce_scatter x1, waiting for transfers between devices, body(): lax.psum_scatter(grad_w_value.astype(jnp.bfloat16), 'items', scatter_dime...  66.2 us
    reduce_scatter x1, waiting for transfers between devices, body(): lax.psum_scatter(grad_w_out.astype(jnp.bfloat16), 'items', scatter_dimens...  54.5 us
    unnamed x13, waiting for transfers between devices  27.9 us
  transfers between devices with their start and end apart: 12, of which 12 were waited for; matrix products, arithmetic and copies ran while one was open for 9% of the time, Pallas kernels for 0%

commit v1 on v0

--- a/solution.py
+++ b/solution.py
@@ -1,6 +1,11 @@
+import functools
+
 import jax
 import jax.numpy as jnp
+import numpy as np
 from jax import lax
+from jax.experimental import pallas as pl
+from jax.experimental.pallas import tpu as pltpu
 from jax.sharding import PartitionSpec as P
 
 HD = 64
@@ -269,36 +274,746 @@
     )
 
 
+MESH = pl.DeviceIdType.MESH
+WIDE = 256
+LOW = jnp.bfloat16
+F32 = jnp.float32
+NEVER = -1e30
+
+
+def dot(left, right):
+    return lax.dot_general(left, right, (((1,), (0,)), ((), ())), preferred_element_type=F32)
+
+
+def dot_nt(left, right):
+    return lax.dot_general(left, right, (((1,), (1,)), ((), ())), preferred_element_type=F32)
+
+
+def dot_tn(left, right):
+    return lax.dot_general(left, right, (((0,), (0,)), ((), ())), preferred_element_type=F32)
+
+
+def rope_constants(rows):
+    quarter = HD // 4
+    freq = 10000.0 ** (-np.arange(quarter) / quarter)
+    tables = []
+    for side, length in ((SIDE_S, SIDE_S * SIDE_S + 1), (SIDE_L, SIDE_L * SIDE_L + 1)):
+        place = np.arange(rows) - 1
+        place = np.where((place >= 0) & (place < length - 1), place, 0)
+        row = (place // side)[:, None] * freq
+        col = (place % side)[:, None] * freq
+        cosine = np.concatenate([np.cos(row), np.cos(row), np.cos(col), np.cos(col)], -1)
+        sine = np.concatenate([-np.sin(row), np.sin(row), -np.sin(col), np.sin(col)], -1)
+        tables += [np.concatenate([cosine, cosine], -1), np.concatenate([sine, sine], -1)]
+    return np.stack(tables).astype(np.float32)
+
+
+def swap_quarters(values):
+    lane = lax.broadcasted_iota(jnp.int32, values.shape, 1)
+    first = (lane % (HD // 2)) < HD // 4
+    return jnp.where(
+        first, pltpu.roll(values, 2 * HD - HD // 4, 1), pltpu.roll(values, HD // 4, 1)
+    )
+
+
+def fused(geo, *refs):
+    rows_here, width, hidden_all = geo
+    (
+        lens, gain_a, gain_f, x_hbm, cot_hbm, tab_hbm,
+        wq, wk, wv, wo, wg, wu, wd,
+        bo_hbm, gi_hbm, fa_hbm, fd_hbm, fq_hbm, gain_hbm,
+        x4, cot4, tab, wqkv_v, wo_v, wg_v, wu_v, wd_v,
+        nrm, nrm_t, qkv, chance, mix_own, mix_in, mix, mix_t,
+        mid, nf, nf_t, hid, hid_t, gg, gu, big,
+        gnf_out, gnf_in, sb, rb, bo, bo_in, gb, gmx, ds_s, gqkv, sb2, rb2, gi, gi_in,
+        gain_s, gain_x, gain_y, gain_z, gain_c,
+        pa, r1a, r2a, r3a, fa, pd, r1d, r2d, r3d, fd, pq, r1q, r2q, r3q, fq,
+        sem_w, sem_in_s, sem_in_r, sem_core_s, sem_core_r, sem_gain_s, sem_gain_r, sem_o,
+        sa_s, sa_r, sd_s, sd_r, sq_s, sq_r,
+    ) = refs
+    s = lax.axis_index("seq")
+    i = lax.axis_index("items")
+    y, c = s // 2, s % 2
+    z, x = i // 2, i % 2
+    rows = 4 * rows_here
+    half = width // 2
+    ff = hidden_all // 2
+    pairs = half // 128
+    step = 32
+    per = rows_here // step
+    blocks = [(r0, min(256, rows - r0)) for r0 in range(0, rows, 256)]
+
+    def device(y_to, c_to, z_to, x_to):
+        return (y_to * 2 + c_to, z_to * 2 + x_to)
+
+    sibling = device(y, 1 - c, z, x)
+    y_dev = device(1 - y, c, z, x)
+    x_dev = device(y, c, z, 1 - x)
+    z_devs = [device(y, c, lax.rem(z + d, 4), x) for d in (1, 2, 3)]
+
+    started = []
+
+    def send(src, dst, s_sem, r_sem, to):
+        return pltpu.make_async_remote_copy(
+            src_ref=src, dst_ref=dst, send_sem=s_sem, recv_sem=r_sem,
+            device_id=to, device_id_type=MESH,
+        )
+
+    def weight_copies():
+        copies = [pltpu.make_async_copy(tab_hbm, tab, sem_w.at[0])]
+        mine = pl.ds(pl.multiple_of(c * half, half), half)
+        for t, w in enumerate((wq, wk, wv)):
+            copies.append(
+                pltpu.make_async_copy(
+                    w.at[:, mine], wqkv_v.at[:, pl.ds(t * half, half)], sem_w.at[1 + t]
+                )
+            )
+        copies.append(pltpu.make_async_copy(wo, wo_v, sem_w.at[4]))
+        for b in range(ff // 128):
+            far = pl.ds(pl.multiple_of(256 * b + 128 * c, 128), 128)
+            near = pl.ds(128 * b, 128)
+            copies.append(pltpu.make_async_copy(wg.at[:, far], wg_v.at[:, near], sem_w.at[5 + 3 * b]))
+            copies.append(pltpu.make_async_copy(wu.at[:, far], wu_v.at[:, near], sem_w.at[6 + 3 * b]))
+            copies.append(pltpu.make_async_copy(wd.at[far], wd_v.at[near], sem_w.at[7 + 3 * b]))
+        return copies
+
+    weights = weight_copies()
+    own_x = pltpu.make_async_copy(x_hbm.at[y], x4.at[s], sem_o.at[0])
+    own_cot = pltpu.make_async_copy(cot_hbm.at[y], cot4.at[s], sem_o.at[1])
+    own_x.start()
+    for copy in weights[:4]:
+        copy.start()
+
+    barrier = pltpu.get_barrier_semaphore()
+    for to in [sibling, y_dev, x_dev] + z_devs:
+        pl.semaphore_signal(barrier, inc=1, device_id=to, device_id_type=MESH)
+    pl.semaphore_wait(barrier, 6)
+
+    s_y = (1 - y) * 2 + c
+    across_x = send(x_hbm.at[1 - y], x4.at[s], sem_in_s.at[0], sem_in_r.at[0], y_dev)
+    beside_x = send(x_hbm.at[y], x4.at[s], sem_in_s.at[1], sem_in_r.at[1], sibling)
+    across_x.start()
+    beside_x.start()
+    across_c = send(cot_hbm.at[1 - y], cot4.at[s], sem_in_s.at[2], sem_in_r.at[2], y_dev)
+    beside_c = send(cot_hbm.at[y], cot4.at[s], sem_in_s.at[3], sem_in_r.at[3], sibling)
+    across_c.start()
+    beside_c.start()
+    own_cot.start()
+    for copy in weights[4:]:
+        copy.start()
+    relay_x = send(x4.at[s_y], x4.at[s_y], sem_in_s.at[4], sem_in_r.at[4], sibling)
+    relay_c = send(cot4.at[s_y], cot4.at[s_y], sem_in_s.at[5], sem_in_r.at[5], sibling)
+
+    length = lens[y]
+
+    def norm_rows(piece):
+        def one(b, carry):
+            here = pl.ds(pl.multiple_of(b * step, step), step)
+            values = x4[piece, here, :].astype(F32)
+            scale = lax.rsqrt(jnp.mean(values * values, -1, keepdims=True) + epsilon)
+            there = pl.ds(pl.multiple_of(piece * rows_here + b * step, step), step)
+            nrm[there, :] = (values * scale * gain_a[...]).astype(LOW)
+            return carry
+
+        lax.fori_loop(0, per, one, 0)
+
+    def project_rows(part):
+        base = pl.multiple_of(part * 2 * rows_here, 32)
+        here = pl.ds(base, 2 * rows_here)
+        cosine = jnp.where(length == LONG, tab[2, here, :], tab[0, here, :])
+        sine = jnp.where(length == LONG, tab[3, here, :], tab[1, here, :])
+        for t in range(3):
+            product = dot(nrm[here, :], wqkv_v[:, t * half : (t + 1) * half])
+            for p in range(pairs):
+                lanes = product[:, 128 * p : 128 * (p + 1)]
+                if t < 2:
+                    lanes = lanes * cosine + swap_quarters(lanes) * sine
+                if t == 0:
+                    lanes = lanes.astype(LOW).astype(F32) * HD ** (-0.5)
+                qkv[t, here, 128 * p : 128 * (p + 1)] = lanes.astype(LOW)
+
+    own_x.wait()
+    norm_rows(s)
+    beside_x.wait_recv()
+    norm_rows(2 * y + 1 - c)
+    for copy in weights[:4]:
+        copy.wait()
+    project_rows(y)
+    across_x.wait_recv()
+    relay_x.start()
+    norm_rows(s_y)
+    relay_x.wait_recv()
+    norm_rows(2 * (1 - y) + 1 - c)
+    project_rows(1 - y)
+
+    lane = lax.broadcasted_iota(jnp.int32, (1, 128), 1)
+    left_head = lane < HD
+    masks = [(lane // HD == n).astype(F32).astype(LOW) for n in range(2)]
+
+    def mix_copy(pair):
+        return send(
+            mix_own.at[pair], mix_in.at[pair], sem_core_s.at[pair], sem_core_r.at[pair], sibling
+        )
+
+    def attend(pair, carry):
+        lanes = pl.ds(pl.multiple_of(pair * 128, 128), 128)
+        for r0, rb in blocks:
+            nk = r0 + rb
+            row = r0 + lax.broadcasted_iota(jnp.int32, (rb, nk), 0)
+            col = lax.broadcasted_iota(jnp.int32, (rb, nk), 1)
+            allowed = (col <= row) & (col < length)
+            both = []
+            for n in range(2):
+                query = qkv[0, r0:nk, lanes] * masks[n]
+                scores = jnp.where(allowed, dot_nt(query, qkv[1, :nk, lanes]), NEVER)
+                expo = jnp.exp(scores - jnp.max(scores, -1, keepdims=True))
+                low = (expo * (1.0 / jnp.sum(expo, -1, keepdims=True))).astype(LOW)
+                chance[pair * 2 + n, r0:nk, :nk] = low
+                both.append(dot(low, qkv[2, :nk, lanes]))
+            mix_own[pair, r0:nk, :] = jnp.where(left_head, both[0], both[1]).astype(LOW)
+        mix_copy(pair).start()
+        return carry
+
+    lax.fori_loop(0, pairs, attend, 0)
+
+    across_c.wait_recv()
+    relay_c.start()
+
+    def turn_rows(src, dst):
+        def one(b, carry):
+            here = pl.ds(pl.multiple_of(b * 128, 128), 128)
+            dst[:, here] = src[here, :].T
+            return carry
+
+        lax.fori_loop(0, rows // 128, one, 0)
+
+    def place_mix(src, at):
+        def one(p, carry):
+            mix[:, pl.ds(pl.multiple_of(at * half + p * 128, 128), 128)] = src[p]
+            return carry
+
+        lax.fori_loop(0, pairs, one, 0)
+
+    place_mix(mix_own, c)
+    turn_rows(nrm, nrm_t)
+    for p in range(pairs):
+        mix_copy(p).wait_recv()
+    place_mix(mix_in, 1 - c)
+
+    weights[4].wait()
+
+    def chunk(n, wide=WIDE):
+        return pl.ds(pl.multiple_of(n * wide, wide), wide)
+
+    def out_project(n, carry):
+        mid[:, chunk(n)] = (
+            dot(mix[...], wo_v[:, chunk(n)])
+            + x4[:, :, chunk(n)].reshape(rows, WIDE).astype(F32)
+        )
+        return carry
+
+    lax.fori_loop(0, width // WIDE, out_project, 0)
+
+    def second_norm(b, carry):
+        here = pl.ds(pl.multiple_of(b * step, step), step)
+        values = mid[here, :]
+        scale = lax.rsqrt(jnp.mean(values * values, -1, keepdims=True) + epsilon)
+        nf[here, :] = (values * scale * gain_f[...]).astype(LOW)
+        return carry
+
+    lax.fori_loop(0, rows // step, second_norm, 0)
+    turn_rows(nf, nf_t)
+    for copy in weights[5:]:
+        copy.wait()
+    own_cot.wait()
+    beside_c.wait_recv()
+    relay_c.wait_recv()
+
+    class Group:
+        def __init__(self, parts, r1, r2, r3, fin, s_sem, r_sem):
+            self.parts, self.r1, self.r2, self.r3, self.fin = parts, r1, r2, r3, fin
+            self.s_sem, self.r_sem = s_sem, r_sem
+
+        def copy1(self, k, x_first):
+            src = self.parts.at[k, :, 1 - x] if x_first else self.parts.at[k, :, :, 1 - y]
+            to = x_dev if x_first else y_dev
+            return send(src, self.r1.at[k], self.s_sem.at[k, 0], self.r_sem.at[k, 0], to)
+
+        def copy2(self, k, x_first):
+            src = self.r1.at[k, :, 1 - y] if x_first else self.r1.at[k, :, 1 - x]
+            to = y_dev if x_first else x_dev
+            return send(src, self.r2.at[k], self.s_sem.at[k, 1], self.r_sem.at[k, 1], to)
+
+        def copy3(self, k, d):
+            return send(
+                self.r2.at[k, lax.rem(z + d, 4)], self.r3.at[k, d - 1],
+                self.s_sem.at[k, 1 + d], self.r_sem.at[k, 1 + d], z_devs[d - 1],
+            )
+
+        def copy4(self, k, n):
+            at = self.fin.at[k, c, y] if n < 2 else self.fin.at[k, c, 1 - y]
+            to = y_dev if n == 0 else sibling
+            return send(at, at, self.s_sem.at[k, 5 + n], self.r_sem.at[k, 5 + n], to)
+
+        def step1(self, k, x_first):
+            self.copy1(k, x_first).start()
+
+        def step2(self, k, x_first):
+            self.copy1(k, x_first).wait_recv()
+
+            def add(other):
+                for zz in range(4):
+                    if x_first:
+                        h = 1 - y if other else y
+                        at, own = (k, zz, h), (k, zz, x, h)
+                    else:
+                        xx = 1 - x if other else x
+                        at, own = (k, zz, xx), (k, zz, xx, y)
+                    self.r1[at] = (self.r1[at].astype(F32) + self.parts[own].astype(F32)).astype(LOW)
+
+            add(True)
+            self.copy2(k, x_first).start()
+            add(False)
+
+        def step3(self, k, x_first):
+            self.copy2(k, x_first).wait_recv()
+            at = y if x_first else x
+            for d in (1, 2, 3, 0):
+                to = lax.rem(z + d, 4)
+                self.r2[k, to] = (
+                    self.r2[k, to].astype(F32) + self.r1[k, to, at].astype(F32)
+                ).astype(LOW)
+                if d:
+                    self.copy3(k, d).start()
+
+        def step4(self, k, x_first):
+            total = self.r2[k, z].astype(F32)
+            for d in (1, 2, 3):
+                self.copy3(k, d).wait_recv()
+                total = total + self.r3[k, d - 1].astype(F32)
+            self.fin[k, c, y] = total.astype(LOW)
+            self.copy4(k, 0).start()
+            self.copy4(k, 1).start()
+
+        def step5(self, k, x_first):
+            self.copy4(k, 0).wait_recv()
+            self.copy4(k, 2).start()
+
+        def step6(self, k, x_first):
+            self.copy4(k, 1).wait_recv()
+            self.copy4(k, 2).wait_recv()
+
+        def sent(self, k, x_first):
+            self.copy1(k, x_first).wait_send()
+            self.copy2(k, x_first).wait_send()
+            for d in (1, 2, 3):
+                self.copy3(k, d).wait_send()
+            for n in range(3):
+                self.copy4(k, n).wait_send()
+
+    group_a = Group(pa, r1a, r2a, r3a, fa, sa_s, sa_r)
+    group_d = Group(pd, r1d, r2d, r3d, fd, sd_s, sd_r)
+    group_q = Group(pq, r1q, r2q, r3q, fq, sq_s, sq_r)
+    chunks_f = ff // WIDE
+    chunks_w = width // WIDE
+
+    def feed(n, carry):
+        at = chunk(n)
+        big[:, 0:WIDE] = dot(nf[...], wg_v[:, at])
+        big[:, WIDE : 2 * WIDE] = dot(nf[...], wu_v[:, at])
+        big[:, 2 * WIDE : 3 * WIDE] = dot_nt(cot4[...].reshape(rows, width), wd_v[at, :])
+
+        def one(b, inner):
+            here = pl.ds(pl.multiple_of(b * step, step), step)
+            gate = big[here, 0:WIDE]
+            up = big[here, WIDE : 2 * WIDE]
+            back = big[here, 2 * WIDE : 3 * WIDE]
+            sigma = 0.5 * jnp.tanh(0.5 * gate) + 0.5
+            silu = gate * sigma
+            hid[here, at] = (silu * up).astype(LOW)
+            gg[here, at] = (back * up * (sigma + silu * (1.0 - sigma))).astype(LOW)
+            gu[here, at] = (back * silu).astype(LOW)
+            return inner
+
+        lax.fori_loop(0, rows // step, one, 0)
+        shape = pa.shape[1:]
+        pa[n] = dot(nf_t[...], gg[:, at]).reshape(shape).astype(LOW)
+        group_a.step1(n, True)
+        pa[n + chunks_f] = dot(nf_t[...], gu[:, at]).reshape(shape).astype(LOW)
+        group_a.step1(n + chunks_f, False)
+        hid_t[at, :] = hid[:, at].T
+        return carry
+
+    lax.fori_loop(0, chunks_f, feed, 0)
+
+    def gnf_copy(n):
+        return send(
+            gnf_out.at[n], gnf_in.at[n], sem_core_s.at[pairs + n], sem_core_r.at[pairs + n], sibling
+        )
+
+    def back_ffn(n, carry):
+        partial = dot_nt(gg[...], wg_v[chunk(n), :]) + dot_nt(gu[...], wu_v[chunk(n), :])
+        big[:, chunk(n)] = partial
+        gnf_out[n] = partial.astype(LOW)
+        gnf_copy(n).start()
+        return carry
+
+    lax.fori_loop(0, chunks_w, back_ffn, 0)
+
+    def down(n, carry):
+        big[:, chunk(n + chunks_w)] = dot(hid[...], wd_v[:, chunk(n)])
+        return carry
+
+    lax.fori_loop(0, chunks_w, down, 0)
+    n_core = pairs + chunks_w
+    bo_copy = send(sb, rb, sem_core_s.at[n_core], sem_core_r.at[n_core], sibling)
+    far = slice(width, 2 * width)
+
+    def for_rows(core, fn):
+        for yy in range(2):
+            def one(b, carry, yy=yy):
+                base = pl.multiple_of((2 * yy + core) * rows_here + b * step, step)
+                fn(yy, b, pl.ds(base, step), pl.ds(pl.multiple_of(b * step, step), step))
+                return carry
+
+            lax.fori_loop(0, per, one, 0)
+
+    def pack_bo(yy, b, here, there):
+        sb[yy, there, :] = big[here, far].astype(LOW)
+
+    for_rows(1 - c, pack_bo)
+    bo_copy.start()
+
+    d_first = [n % 2 == 0 for n in range(chunks_w)]
+
+    for n in range(chunks_w):
+        at = slice(n * WIDE, (n + 1) * WIDE)
+        pd[n] = (
+            dot(hid_t[...], cot4[:, :, at].reshape(rows, WIDE)).reshape(pd.shape[1:]).astype(LOW)
+        )
+        group_d.step1(n, d_first[n])
+
+    bo_copy.wait_recv()
+
+    def finish_bo(yy, b, here, there):
+        bo[yy, there, :] = (mid[here, :] + big[here, far] + rb[yy, there, :].astype(F32)).astype(LOW)
+
+    for_rows(c, finish_bo)
+    bo_across = send(bo.at[1 - y], bo_in, sem_in_s.at[6], sem_in_r.at[6], y_dev)
+    bo_across.start()
+
+    for n in range(chunks_w):
+        gnf_copy(n).wait_recv()
+
+    def middle_back(b, total):
+        here = pl.ds(pl.multiple_of(b * step, step), step)
+        values = mid[here, :]
+        grad = big[here, 0:width] + jnp.concatenate(
+            [gnf_in[n, here, :].astype(F32) for n in range(chunks_w)], -1
+        )
+        scale = lax.rsqrt(jnp.mean(values * values, -1, keepdims=True) + epsilon)
+        unit = values * scale
+        total = total + (grad * unit).reshape(step // 8, 8, width).sum(0)
+        scaled = grad * gain_f[...]
+        inner = jnp.mean(scaled * unit, -1, keepdims=True)
+        out = cot4[b // per, pl.ds(pl.multiple_of(lax.rem(b, per) * step, step), step), :].astype(F32)
+        out = out + scale * (scaled - unit * inner)
+        mid[here, :] = out
+        gb[here, :] = out.astype(LOW)
+        return total
+
+    total_f = lax.fori_loop(0, rows // step, middle_back, jnp.zeros((8, width), F32))
+
+    turn_rows(mix, mix_t)
+    mine = pl.ds(pl.multiple_of(c * half, half), half)
+    pq[0] = dot(mix_t[...], gb[:, mine]).reshape(pq.shape[1:]).astype(LOW)
+    group_q.step1(0, True)
+    gmx[...] = dot_nt(gb[...], wo_v[mine, :]).astype(LOW)
+
+    def attend_back(pair, carry):
+        lanes = pl.ds(pl.multiple_of(pair * 128, 128), 128)
+
+        def keep(n, at, off, value):
+            where_ = pl.ds(pl.multiple_of(off * 128, 128), 128)
+            if n:
+                value = jnp.where(left_head, big[at, where_], value)
+            big[at, where_] = value
+
+        for n in range(2):
+            head = pair * 2 + n
+            for r0, rb_ in blocks:
+                nk = r0 + rb_
+                grad = gmx[r0:nk, lanes] * masks[n]
+                prob = chance[head, r0:nk, :nk].astype(F32)
+                each = dot_nt(grad, qkv[2, :nk, lanes]) * prob
+                low = (each - prob * jnp.sum(each, -1, keepdims=True)).astype(LOW)
+                ds_s[r0:nk, :nk] = low
+                keep(n, slice(r0, nk), 0, dot(low, qkv[1, :nk, lanes]))
+            for k0, kb in blocks:
+                at = slice(k0, k0 + kb)
+                keep(n, at, 1, dot_tn(ds_s[k0:, at], qkv[0, k0:, lanes]))
+                keep(n, at, 2, dot_tn(chance[head, k0:, at], gmx[k0:, lanes]))
+
+        def one(b, inner):
+            here = pl.ds(pl.multiple_of(b * 64, 64), 64)
+            cosine = jnp.where(length == LONG, tab[2, here, :], tab[0, here, :])
+            sine = jnp.where(length == LONG, tab[3, here, :], tab[1, here, :])
+            for t in range(3):
+                values = big[here, 128 * t : 128 * (t + 1)]
+                if t == 0:
+                    values = values * HD ** (-0.5)
+                if t < 2:
+                    values = values * cosine - swap_quarters(values) * sine
+                gqkv[here, pl.ds(pl.multiple_of(t * half + pair * 128, 128), 128)] = values.astype(LOW)
+            return inner
+
+        lax.fori_loop(0, rows // 64, one, 0)
+        return carry
+
+    lax.fori_loop(0, pairs, attend_back, 0)
+
+    q_first = [True, True, False, True]
+    for t in range(3):
+        pq[1 + t] = (
+            dot(nrm_t[...], gqkv[:, t * half : (t + 1) * half]).reshape(pq.shape[1:]).astype(LOW)
+        )
+        group_q.step1(1 + t, q_first[1 + t])
+
+    def back_attn(n, carry):
+        big[:, chunk(n)] = dot_nt(gqkv[...], wqkv_v[chunk(n), :])
+        return carry
+
+    lax.fori_loop(0, chunks_w, back_attn, 0)
+
+    def pack_gi(yy, b, here, there):
+        sb2[yy, there, :] = big[here, 0:width].astype(LOW)
+
+    for_rows(1 - c, pack_gi)
+    gi_copy = send(sb2, rb2, sem_core_s.at[n_core + 1], sem_core_r.at[n_core + 1], sibling)
+    gi_copy.start()
+
+    def gain_back(b, total):
+        here = pl.ds(pl.multiple_of(b * step, step), step)
+        values = x4[b // per, pl.ds(pl.multiple_of(lax.rem(b, per) * step, step), step), :].astype(F32)
+        scale = lax.rsqrt(jnp.mean(values * values, -1, keepdims=True) + epsilon)
+        return total + (big[here, 0:width] * (values * scale)).reshape(step // 8, 8, width).sum(0)
+
+    total_a = lax.fori_loop(0, rows // step, gain_back, jnp.zeros((8, width), F32))
+    gain_s[...] = jnp.concatenate(
+        [
+            jnp.broadcast_to(jnp.sum(total_a, 0, keepdims=True), (8, width)),
+            jnp.broadcast_to(jnp.sum(total_f, 0, keepdims=True), (8, width)),
+        ],
+        0,
+    )
+    gain_1 = send(gain_s, gain_x, sem_gain_s.at[0], sem_gain_r.at[0], x_dev)
+    gain_1.start()
+    gi_copy.wait_recv()
+
+    def finish_gi(yy, b, here, there):
+        values = x4[2 * yy + c, there, :].astype(F32)
+        scale = lax.rsqrt(jnp.mean(values * values, -1, keepdims=True) + epsilon)
+        unit = values * scale
+        scaled = (big[here, 0:width] + rb2[yy, there, :].astype(F32)) * gain_a[...]
+        inner = jnp.mean(scaled * unit, -1, keepdims=True)
+        gi[yy, there, :] = (mid[here, :] + scale * (scaled - unit * inner)).astype(LOW)
+
+    for_rows(c, finish_gi)
+    gi_across = send(gi.at[1 - y], gi_in, sem_in_s.at[7], sem_in_r.at[7], y_dev)
+    gi_across.start()
+
+    todo = []
+    for n in range(chunks_f):
+        todo += [(group_a, n, True), (group_a, n + chunks_f, False)]
+    todo += [(group_d, n, d_first[n]) for n in range(chunks_w)]
+    todo += [(group_q, n, q_first[n]) for n in range(4)]
+    lag = 4
+    names = ["step2", "step3", "step4", "step5", "step6"]
+    for tick in range(len(todo) + lag * (len(names) - 1)):
+        for stage in range(len(names) - 1, -1, -1):
+            at = tick - lag * stage
+            if 0 <= at < len(todo):
+                group, k, first = todo[at]
+                getattr(group, names[stage])(k, first)
+
+    gain_1.wait()
+    gain_s[...] = gain_s[...] + gain_x[...]
+    gain_2 = send(gain_s, gain_y, sem_gain_s.at[1], sem_gain_r.at[1], y_dev)
+    gain_2.start()
+    gain_2.wait()
+    gain_s[...] = gain_s[...] + gain_y[...]
+    gain_3 = [
+        send(gain_s, gain_z.at[d], sem_gain_s.at[2 + d], sem_gain_r.at[2 + d], z_devs[d])
+        for d in range(3)
+    ]
+    for copy in gain_3:
+        copy.start()
+    for copy in gain_3:
+        copy.wait()
+    gain_s[...] = gain_s[...] + gain_z[0] + gain_z[1] + gain_z[2]
+    gain_4 = send(gain_s, gain_c, sem_gain_s.at[5], sem_gain_r.at[5], sibling)
+    gain_4.start()
+    gain_4.wait()
+    gain_c[0:8, :] = gain_s[0:8, :] + gain_c[0:8, :]
+
+    outs = [
+        pltpu.make_async_copy(fa, fa_hbm, sem_o.at[2]),
+        pltpu.make_async_copy(fd, fd_hbm, sem_o.at[3]),
+        pltpu.make_async_copy(fq, fq_hbm, sem_o.at[4]),
+        pltpu.make_async_copy(gain_c, gain_hbm, sem_o.at[5]),
+        pltpu.make_async_copy(bo.at[y], bo_hbm.at[y], sem_o.at[6]),
+        pltpu.make_async_copy(gi.at[y], gi_hbm.at[y], sem_o.at[7]),
+    ]
+    for copy in outs:
+        copy.start()
+    bo_across.wait_recv()
+    gi_across.wait_recv()
+    outs += [
+        pltpu.make_async_copy(bo_in, bo_hbm.at[1 - y], sem_o.at[8]),
+        pltpu.make_async_copy(gi_in, gi_hbm.at[1 - y], sem_o.at[9]),
+    ]
+    for copy in outs[6:]:
+        copy.start()
+    for copy in outs:
+        copy.wait()
+
+    for copy in (across_x, beside_x, across_c, beside_c, relay_x, relay_c, bo_across, gi_across):
+        copy.wait_send()
+    for p in range(pairs):
+        mix_copy(p).wait_send()
+    for n in range(chunks_w):
+        gnf_copy(n).wait_send()
+    bo_copy.wait_send()
+    gi_copy.wait_send()
+    for group, k, first in todo:
+        group.sent(k, first)
+
+
+def spread(chunks_f, fa, fd, fq, bo, gi, bo_out, gi_out, dq, dk, dv, do, dg, du, dd):
+    bo_out[...] = bo[...]
+    gi_out[...] = gi[...]
+    rows = fa.shape[3]
+    for core in range(2):
+        for h in range(2):
+            at = slice(h * rows, (h + 1) * rows)
+            for n in range(chunks_f):
+                for b in range(WIDE // 128):
+                    far = 256 * (n * (WIDE // 128) + b) + 128 * core
+                    near = slice(128 * b, 128 * (b + 1))
+                    dg[at, far : far + 128] = fa[n, core, h, :, near].astype(F32)
+                    du[at, far : far + 128] = fa[n + chunks_f, core, h, :, near].astype(F32)
+            half = fq.shape[4]
+            lanes = slice(core * half, (core + 1) * half)
+            for n, ref in enumerate((do, dq, dk, dv)):
+                ref[at, lanes] = fq[n, core, h].astype(F32)
+            deep = fd.shape[3]
+            at = slice((2 * core + h) * deep, (2 * core + h + 1) * deep)
+            for n in range(fd.shape[0]):
+                dd[at, WIDE * n : WIDE * (n + 1)] = fd[n, core, h].astype(F32)
+
+
+def item_per_chip(
+    block_in, lengths, gain_attn, w_query, w_key, w_value, w_out, gain_ffn, w_gate, w_up, w_down,
+    cotangent,
+):
+    _, rows_here, width = block_in.shape
+    hidden_all = w_gate.shape[1]
+    rows = rows_here * lax.axis_size("seq")
+    shares = lax.axis_size("items")
+    half, ff = width // 2, hidden_all // 2
+    pairs = half // 128
+    chunks_f, chunks_w = ff // WIDE, width // WIDE
+    thin, deep = width // shares // 2, ff // shares // 2
+    tables = jnp.asarray(rope_constants(rows))
+    any_ = pl.BlockSpec(memory_space=pl.ANY)
+    vmem = pl.BlockSpec(memory_space=pltpu.VMEM)
+
+    def group(n, r, w):
+        return [
+            pltpu.VMEM((n, 4, 2, 2, r, w), LOW),
+            pltpu.VMEM((n, 4, 2, r, w), LOW),
+            pltpu.VMEM((n, 4, r, w), LOW),
+            pltpu.VMEM((n, 3, r, w), LOW),
+            pltpu.VMEM((n, 2, 2, r, w), LOW),
+        ]
+
+    def low(*shape):
+        return pltpu.VMEM(shape, LOW)
+
+    def full(*shape):
+        return pltpu.VMEM(shape, F32)
+
+    dma = pltpu.SemaphoreType.DMA
+    scratch = [
+        low(4, rows_here, width), low(4, rows_here, width), full(4, rows, 128),
+        low(width, 3 * half), low(width, width), low(width, ff), low(width, ff), low(ff, width),
+        low(rows, width), low(width, rows), low(3, rows, half), low(2 * pairs, rows, rows),
+        low(pairs, rows, 128), low(pairs, rows, 128), low(rows, width), low(width, rows),
+        full(rows, width), low(rows, width), low(width, rows), low(rows, ff), low(ff, rows),
+        low(rows, ff), low(rows, ff), full(rows, 2 * width),
+        low(chunks_w, rows, WIDE), low(chunks_w, rows, WIDE),
+        low(2, rows_here, width), low(2, rows_here, width),
+        low(2, rows_here, width), low(rows_here, width),
+        low(rows, width), low(rows, half), low(rows, rows), low(rows, 3 * half),
+        low(2, rows_here, width), low(2, rows_here, width),
+        low(2, rows_here, width), low(rows_here, width),
+        full(16, width), full(16, width), full(16, width), full(3, 16, width), full(16, width),
+    ]
+    scratch += group(2 * chunks_f, thin, WIDE) + group(chunks_w, deep, WIDE) + group(4, thin, half)
+    scratch += [
+        dma((5 + 3 * (ff // 128),)), dma((8,)), dma((8,)),
+        dma((pairs + chunks_w + 2,)), dma((pairs + chunks_w + 2,)), dma((6,)), dma((6,)), dma((10,)),
+        dma((2 * chunks_f, 8)), dma((2 * chunks_f, 8)), dma((chunks_w, 8)), dma((chunks_w, 8)),
+        dma((4, 8)), dma((4, 8)),
+    ]
+    shape = jax.ShapeDtypeStruct
+    bo, gi, fa, fd, fq, gains = pl.pallas_call(
+        functools.partial(fused, (rows_here, width, hidden_all)),
+        out_shape=(
+            shape(block_in.shape, LOW), shape(block_in.shape, LOW),
+            shape((2 * chunks_f, 2, 2, thin, WIDE), LOW), shape((chunks_w, 2, 2, deep, WIDE), LOW),
+            shape((4, 2, 2, thin, half), LOW), shape((16, width), F32),
+        ),
+        in_specs=[pl.BlockSpec(memory_space=pltpu.SMEM), vmem, vmem] + [any_] * 10,
+        out_specs=(any_,) * 6,
+        scratch_shapes=scratch,
+        compiler_params=pltpu.CompilerParams(
+            collective_id=0, has_side_effects=True, vmem_limit_bytes=63 * 2**20
+        ),
+        name="block",
+    )(
+        lengths, gain_attn.reshape(1, width), gain_ffn.reshape(1, width), block_in, cotangent, tables,
+        w_query, w_key, w_value, w_out, w_gate, w_up, w_down,
+    )
+    thick = (width // shares, width)
+    bo, gi, dq, dk, dv, do, dg, du, dd = pl.pallas_call(
+        functools.partial(spread, chunks_f),
+        out_shape=(
+            shape(block_in.shape, LOW), shape(block_in.shape, LOW),
+            shape(thick, F32), shape(thick, F32), shape(thick, F32), shape(thick, F32),
+            shape((width // shares, hidden_all), F32), shape((width // shares, hidden_all), F32),
+            shape((hidden_all // shares, width), F32),
+        ),
+        in_specs=[vmem] * 5,
+        out_specs=(vmem,) * 9,
+        compiler_params=pltpu.CompilerParams(vmem_limit_bytes=32 * 2**20),
+        name="spread",
+    )(fa, fd, fq, bo, gi)
+    share = width // shares
+    gains = lax.dynamic_slice(gains, (0, lax.axis_index("items") * share), (16, share))
+    return bo, gi, gains[0], dq, dk, dv, do, gains[8], dg, du, dd
+
+
 def solution(mesh):
+    fits = mesh.shape["seq"] == 4 and mesh.shape["items"] == 8
     return jax.shard_map(
-        body,
+        item_per_chip if fits else body,
         mesh=mesh,
-        in_specs=(
-            P("items", "seq", None),
-            P("items"),
-            P(),
-            P(),
-            P(),
-            P(),
-            P(),
-            P(),
-            P(),
-            P(),
-            P(),
-            P("items", "seq", None),
-        ),
+        in_specs=(P("items", "seq", None), P("items")) + (P(),) * 9 + (P("items", "seq", None),),
         out_specs=(
-            P("items", "seq", None),
-            P("items", "seq", None),
-            P("items"),
-            P("items", None),
-            P("items", None),
-            P("items", None),
-            P("items", None),
-            P("items"),
-            P("items", None),
-            P("items", None),
-            P("items", None),
+            (P("items", "seq", None),) * 2
+            + (P("items"),) + (P("items", None),) * 4
+            + (P("items"),) + (P("items", None),) * 3
         ),
         check_vma=False,
     )

time: 781 us -> 153 us (0.20); the launches traced: 772 us -> 152 us
  waiting for transfers between devices: 573 us -> 0 us
  Pallas kernels: 0 us -> 143 us
  matrix products: 87 us -> 0 us
  local copies, waits for them, and re-layouts: 39.3 us -> 9.1 us
  other arithmetic: 28 us -> 0 us
  blocking collectives: 26.7 us -> 0 us
  between operations: 16.6 us -> 0.66 us
    reduce_scatter x8 -> x0, waiting for transfers between devices: 499 us -> none  [the longest x1 78.3 us: body(): lax.psum_scatter(grad_w_gate.astype(jnp.bfloat16), 'items', scatter_dimen...]
    pallas_call x0 -> x2, Pallas kernels: none -> 143 us  [the longest x1 140 us: item_per_chip(): pl.pallas_call(functools.partial(fused, (rows_here, width, hidden_all)),...]
    dot_general x27 -> x0, matrix products: 87 us -> none  [the longest x7 24.6 us: weight_grad(): jnp.einsum('ird,ire->de', left, right, preferred_element_type=jnp.float32)]
    all_gather x2 -> x0, waiting for transfers between devices: 28.2 us -> none  [the longest x1 15.8 us: body(): lax.all_gather(keys, 'seq', axis=1, tiled=True)]
    unnamed x13 -> x0, waiting for transfers between devices: 27.9 us -> none
    psum x1 -> x0, waiting for transfers between devices: 18.2 us -> none  [body(): lax.psum(shares[1].astype(jnp.bfloat16), 'seq').astype(jnp.float32)]
    convert_element_type x16 -> x0, other arithmetic: 17.8 us -> none  [the longest x1 2.71 us: body(): keys = (keys_pre * cosine + turn(keys_pre) * sine).astype(jnp.bfloat16).r...]
    unnamed x1 -> x0, blocking collectives: 15.7 us -> none
  transfers between devices with their start and end apart: 12 -> 0, of which waited for: 12 -> 0; matrix products, arithmetic and copies ran while one was open for 9% -> 0% of each run, Pallas kernels for 0% -> 0%
where the time goes in v1:
time: 153 us; the launch traced here: 152 us
  Pallas kernels  143 us (93%)
  local copies, waits for them, and re-layouts  9.1 us (6%)
    pallas_call x1, Pallas kernels, item_per_chip(): pl.pallas_call(functools.partial(fused, (rows_here, width, hidden_all)),...  140 us
    unnamed x10, local copies, waits for them, and re-layouts  5.25 us

profile of v1, /device:TPU:1, one launch (start us, length us, event | category | flops | bytes accessed | tf_op | source)
XLA Modules:
  0.0 152.3 jit_solution(1561833362318471861)
XLA Ops:
  0.6 1.3 reshape.28.refs_1_
  1.9 1.3 reshape.29.refs_2_
  3.2 140.4 %block.1 = (bf16[2,160,768]{2,1,0:T(8,128)(2,1)}, bf16[2,160,768]{2,1,0:T(8,128)(2,1)}, bf16[8,2,2,48,256]{4,3,2,1,0:T(8,128)(2,1)}, bf16[3,2,2,64,256]{4,3,2,1,...) custom-call(s32[2]{0:T(128)} %refs_0_.1, f32[1,768]{1,0:T(1,128)} %reshape.28.refs_1_, ...), custom_call_target="tpu_custom_call" | custom-call | tf_op jit(solution)/shard_map/block/pallas_call | solution.py:970
  143.6 1.3 dynamic-slice_bitcast_fusion
  144.9 0.0 copy-start
  144.9 1.1 copy-done
  146.0 0.0 copy-start.1
  146.0 1.1 copy-done.1
  147.1 0.0 copy-start.2
  147.1 1.0 copy-done.2
  148.1 0.0 copy-start.3
  148.1 1.0 copy-done.3
  149.2 0.0 copy-start.4
  149.2 1.0 copy-done.4
  150.2 2.2 %spread.1 = (bf16[2,160,768]{2,1,0:T(8,128)(2,1)}, bf16[2,160,768]{2,1,0:T(8,128)(2,1)}, f32[96,768]{1,0:T(8,128)}, f32[96,768]{1,0:T(8,128)}, f32[96,768]{1,0:T...) custom-call(bf16[8,2,2,48,256]{4,3,2,1,0:T(8,128)(2,1)S(1)} %copy-done, ...), custom_call_target="tpu_custom_call" | custom-call | tf_op jit(solution)/shard_map/spread/pallas_call | solution.py:989
Async XLA Ops:
  144.9 1.1 copy-start
  146.0 1.1 copy-start.1
  147.1 1.0 copy-start.2
  148.1 1.0 copy-start.3
  149.2 1.0 copy-start.4

commit v2 on v1

--- a/solution.py
+++ b/solution.py
@@ -280,6 +280,29 @@
 F32 = jnp.float32
 NEVER = -1e30
 
+ORDER = (
+    (2, 42),
+    (12, 52),
+    (),
+    (),
+    (22, 62),
+    (3,),
+    (),
+    (),
+    (32, 72),
+    (13, 43, 53, 82, 63),
+    (23,),
+    (92, 112, 33, 73, 44),
+    (54, 102),
+    (83, 4),
+    (64,),
+    (93,),
+    (
+        14, 24, 34, 122, 45, 55, 113, 103, 74, 132, 84, 94, 133, 142, 65, 123, 143, 104, 114, 134,
+        75, 85, 95, 124, 105, 144, 135, 145,
+    ),
+)
+
 
 def dot(left, right):
     return lax.dot_general(left, right, (((1,), (0,)), ((), ())), preferred_element_type=F32)
@@ -339,7 +362,8 @@
     half = width // 2
     ff = hidden_all // 2
     pairs = half // 128
-    step = 32
+    step = rows_here
+    fine = 32
     per = rows_here // step
     blocks = [(r0, min(256, rows - r0)) for r0 in range(0, rows, 256)]
 
@@ -396,8 +420,6 @@
     beside_x.start()
     across_c = send(cot_hbm.at[1 - y], cot4.at[s], sem_in_s.at[2], sem_in_r.at[2], y_dev)
     beside_c = send(cot_hbm.at[y], cot4.at[s], sem_in_s.at[3], sem_in_r.at[3], sibling)
-    across_c.start()
-    beside_c.start()
     own_cot.start()
     for copy in weights[4:]:
         copy.start()
@@ -441,6 +463,8 @@
     project_rows(y)
     across_x.wait_recv()
     relay_x.start()
+    across_c.start()
+    beside_c.start()
     norm_rows(s_y)
     relay_x.wait_recv()
     norm_rows(2 * (1 - y) + 1 - c)
@@ -534,86 +558,145 @@
             self.parts, self.r1, self.r2, self.r3, self.fin = parts, r1, r2, r3, fin
             self.s_sem, self.r_sem = s_sem, r_sem
 
-        def copy1(self, k, x_first):
-            src = self.parts.at[k, :, 1 - x] if x_first else self.parts.at[k, :, :, 1 - y]
-            to = x_dev if x_first else y_dev
-            return send(src, self.r1.at[k], self.s_sem.at[k, 0], self.r_sem.at[k, 0], to)
-
-        def copy2(self, k, x_first):
-            src = self.r1.at[k, :, 1 - y] if x_first else self.r1.at[k, :, 1 - x]
-            to = y_dev if x_first else x_dev
-            return send(src, self.r2.at[k], self.s_sem.at[k, 1], self.r_sem.at[k, 1], to)
-
-        def copy3(self, k, d):
-            return send(
-                self.r2.at[k, lax.rem(z + d, 4)], self.r3.at[k, d - 1],
-                self.s_sem.at[k, 1 + d], self.r_sem.at[k, 1 + d], z_devs[d - 1],
+        def copy(self, k, n, src, dst, to):
+            return send(src, dst, self.s_sem.at[k, n], self.r_sem.at[k, n], to)
+
+        def add(self, k, to, own):
+            self.r1[to] = (self.r1[to].astype(F32) + self.parts[own].astype(F32)).astype(LOW)
+
+    class ByX(Group):
+        def first(self, k):
+            return self.copy(k, 0, self.parts.at[k, :, 1 - x], self.r1.at[k], x_dev)
+
+        def along_z(self, k, d):
+            return self.copy(
+                k, d, self.r1.at[k, lax.rem(z + d, 4)], self.r2.at[k, pl.ds(2 * d - 2, 2)], z_devs[d - 1]
             )
 
-        def copy4(self, k, n):
+        def over_y(self, k):
+            return self.copy(k, 4, self.r1.at[k, z], self.r3.at[k, pl.ds(0, 2)], y_dev)
+
+        def to_core(self, k):
+            return self.copy(k, 5, self.fin.at[k, c], self.fin.at[k, c], sibling)
+
+        def step1(self, k):
+            self.first(k).start()
+
+        def step2(self, k):
+            self.first(k).wait_recv()
+            for d in (1, 2, 3, 0):
+                to = lax.rem(z + d, 4)
+                for h in range(2):
+                    self.add(k, (k, to, h), (k, to, x, h))
+                if d:
+                    self.along_z(k, d).start()
+
+        def step3(self, k):
+            for d in (1, 2, 3):
+                self.along_z(k, d).wait_recv()
+            for h in range(2):
+                total = self.r1[k, z, h].astype(F32)
+                for d in (1, 2, 3):
+                    total = total + self.r2[k, 2 * d - 2 + h].astype(F32)
+                self.r1[k, z, h] = total.astype(LOW)
+            self.over_y(k).start()
+
+        def step4(self, k):
+            self.over_y(k).wait_recv()
+            for h in range(2):
+                total = self.r1[k, z, h].astype(F32) + self.r3[k, h].astype(F32)
+                self.fin[k, c, h] = total.astype(LOW)
+            self.to_core(k).start()
+
+        def end(self, k):
+            self.to_core(k).wait_recv()
+
+        def sent(self, k):
+            self.first(k).wait_send()
+            for d in (1, 2, 3):
+                self.along_z(k, d).wait_send()
+            self.over_y(k).wait_send()
+            self.to_core(k).wait_send()
+
+    class ByY(Group):
+        def first(self, k):
+            return self.copy(k, 0, self.parts.at[k, :, :, 1 - y], self.r1.at[k], y_dev)
+
+        def second(self, k):
+            return self.copy(k, 1, self.r1.at[k, :, 1 - x], self.r2.at[k, pl.ds(0, 4)], x_dev)
+
+        def along_z(self, k, d):
+            return self.copy(
+                k, 1 + d, self.r2.at[k, lax.rem(z + d, 4)], self.r3.at[k, d - 1], z_devs[d - 1]
+            )
+
+        def copies_out(self, k, n):
             at = self.fin.at[k, c, y] if n < 2 else self.fin.at[k, c, 1 - y]
-            to = y_dev if n == 0 else sibling
-            return send(at, at, self.s_sem.at[k, 5 + n], self.r_sem.at[k, 5 + n], to)
-
-        def step1(self, k, x_first):
-            self.copy1(k, x_first).start()
-
-        def step2(self, k, x_first):
-            self.copy1(k, x_first).wait_recv()
-
-            def add(other):
-                for zz in range(4):
-                    if x_first:
-                        h = 1 - y if other else y
-                        at, own = (k, zz, h), (k, zz, x, h)
-                    else:
-                        xx = 1 - x if other else x
-                        at, own = (k, zz, xx), (k, zz, xx, y)
-                    self.r1[at] = (self.r1[at].astype(F32) + self.parts[own].astype(F32)).astype(LOW)
-
-            add(True)
-            self.copy2(k, x_first).start()
-            add(False)
-
-        def step3(self, k, x_first):
-            self.copy2(k, x_first).wait_recv()
-            at = y if x_first else x
+            return self.copy(k, 5 + n, at, at, y_dev if n == 0 else sibling)
+
+        def step1(self, k):
+            self.first(k).start()
+
+        def step2(self, k):
+            self.first(k).wait_recv()
+            for zz in range(4):
+                self.add(k, (k, zz, 1 - x), (k, zz, 1 - x, y))
+            self.second(k).start()
+            for zz in range(4):
+                self.add(k, (k, zz, x), (k, zz, x, y))
+
+        def step3(self, k):
+            self.second(k).wait_recv()
             for d in (1, 2, 3, 0):
                 to = lax.rem(z + d, 4)
                 self.r2[k, to] = (
-                    self.r2[k, to].astype(F32) + self.r1[k, to, at].astype(F32)
+                    self.r2[k, to].astype(F32) + self.r1[k, to, x].astype(F32)
                 ).astype(LOW)
                 if d:
-                    self.copy3(k, d).start()
-
-        def step4(self, k, x_first):
+                    self.along_z(k, d).start()
+
+        def step4(self, k):
             total = self.r2[k, z].astype(F32)
             for d in (1, 2, 3):
-                self.copy3(k, d).wait_recv()
+                self.along_z(k, d).wait_recv()
                 total = total + self.r3[k, d - 1].astype(F32)
             self.fin[k, c, y] = total.astype(LOW)
-            self.copy4(k, 0).start()
-            self.copy4(k, 1).start()
-
-        def step5(self, k, x_first):
-            self.copy4(k, 0).wait_recv()
-            self.copy4(k, 2).start()
-
-        def step6(self, k, x_first):
-            self.copy4(k, 1).wait_recv()
-            self.copy4(k, 2).wait_recv()
-
-        def sent(self, k, x_first):
-            self.copy1(k, x_first).wait_send()
-            self.copy2(k, x_first).wait_send()
+            self.copies_out(k, 0).start()
+            self.copies_out(k, 1).start()
+
+        def step5(self, k):
+            self.copies_out(k, 0).wait_recv()
+            self.copies_out(k, 2).start()
+
+        def end(self, k):
+            self.copies_out(k, 1).wait_recv()
+            self.copies_out(k, 2).wait_recv()
+
+        def sent(self, k):
+            self.first(k).wait_send()
+            self.second(k).wait_send()
             for d in (1, 2, 3):
-                self.copy3(k, d).wait_send()
+                self.along_z(k, d).wait_send()
             for n in range(3):
-                self.copy4(k, n).wait_send()
-
-    group_a = Group(pa, r1a, r2a, r3a, fa, sa_s, sa_r)
-    group_d = Group(pd, r1d, r2d, r3d, fd, sd_s, sd_r)
-    group_q = Group(pq, r1q, r2q, r3q, fq, sq_s, sq_r)
+                self.copies_out(k, n).wait_send()
+
+    buffers_a = (pa, r1a, r2a, r3a, fa, sa_s, sa_r)
+    buffers_d = (pd, r1d, r2d, r3d, fd, sd_s, sd_r)
+    buffers_q = (pq, r1q, r2q, r3q, fq, sq_s, sq_r)
+    chunks = [(ByX(*buffers_a), n) for n in range(4)] + [(ByY(*buffers_a), n + 4) for n in range(4)]
+    chunks += [(plan(*buffers_d), n) for n, plan in enumerate((ByY, ByY, ByY))]
+    chunks += [(plan(*buffers_q), n) for n, plan in enumerate((ByX, ByX, ByY, ByY))]
+    slots = iter(ORDER)
+
+    def first(chunk):
+        group, k = chunks[chunk]
+        group.step1(k)
+
+    def turn():
+        for code in next(slots):
+            group, k = chunks[code // 10]
+            getattr(group, f"step{code % 10}")(k)
+
     chunks_f = ff // WIDE
     chunks_w = width // WIDE
 
@@ -624,7 +707,7 @@
         big[:, 2 * WIDE : 3 * WIDE] = dot_nt(cot4[...].reshape(rows, width), wd_v[at, :])
 
         def one(b, inner):
-            here = pl.ds(pl.multiple_of(b * step, step), step)
+            here = pl.ds(pl.multiple_of(b * fine, fine), fine)
             gate = big[here, 0:WIDE]
             up = big[here, WIDE : 2 * WIDE]
             back = big[here, 2 * WIDE : 3 * WIDE]
@@ -635,16 +718,17 @@
             gu[here, at] = (back * silu).astype(LOW)
             return inner
 
-        lax.fori_loop(0, rows // step, one, 0)
+        lax.fori_loop(0, rows // fine, one, 0, unroll=5)
         shape = pa.shape[1:]
         pa[n] = dot(nf_t[...], gg[:, at]).reshape(shape).astype(LOW)
-        group_a.step1(n, True)
+        chunks[0][0].step1(n)
         pa[n + chunks_f] = dot(nf_t[...], gu[:, at]).reshape(shape).astype(LOW)
-        group_a.step1(n + chunks_f, False)
+        chunks[4][0].step1(n + chunks_f)
         hid_t[at, :] = hid[:, at].T
         return carry
 
     lax.fori_loop(0, chunks_f, feed, 0)
+    turn()
 
     def gnf_copy(n):
         return send(
@@ -659,6 +743,7 @@
         return carry
 
     lax.fori_loop(0, chunks_w, back_ffn, 0)
+    turn()
 
     def down(n, carry):
         big[:, chunk(n + chunks_w)] = dot(hid[...], wd_v[:, chunk(n)])
@@ -684,15 +769,15 @@
     for_rows(1 - c, pack_bo)
     bo_copy.start()
 
-    d_first = [n % 2 == 0 for n in range(chunks_w)]
-
     for n in range(chunks_w):
+        turn()
         at = slice(n * WIDE, (n + 1) * WIDE)
         pd[n] = (
             dot(hid_t[...], cot4[:, :, at].reshape(rows, WIDE)).reshape(pd.shape[1:]).astype(LOW)
         )
-        group_d.step1(n, d_first[n])
-
+        first(8 + n)
+
+    turn()
     bo_copy.wait_recv()
 
     def finish_bo(yy, b, here, there):
@@ -702,6 +787,7 @@
     bo_across = send(bo.at[1 - y], bo_in, sem_in_s.at[6], sem_in_r.at[6], y_dev)
     bo_across.start()
 
+    turn()
     for n in range(chunks_w):
         gnf_copy(n).wait_recv()
 
@@ -724,17 +810,18 @@
 
     total_f = lax.fori_loop(0, rows // step, middle_back, jnp.zeros((8, width), F32))
 
+    turn()
     turn_rows(mix, mix_t)
     mine = pl.ds(pl.multiple_of(c * half, half), half)
     pq[0] = dot(mix_t[...], gb[:, mine]).reshape(pq.shape[1:]).astype(LOW)
-    group_q.step1(0, True)
+    first(11)
     gmx[...] = dot_nt(gb[...], wo_v[mine, :]).astype(LOW)
 
     def attend_back(pair, carry):
-        lanes = pl.ds(pl.multiple_of(pair * 128, 128), 128)
+        lanes = slice(pair * 128, pair * 128 + 128)
 
         def keep(n, at, off, value):
-            where_ = pl.ds(pl.multiple_of(off * 128, 128), 128)
+            where_ = slice(off * 128, off * 128 + 128)
             if n:
                 value = jnp.where(left_head, big[at, where_], value)
             big[at, where_] = value
@@ -764,26 +851,31 @@
                     values = values * HD ** (-0.5)
                 if t < 2:
                     values = values * cosine - swap_quarters(values) * sine
-                gqkv[here, pl.ds(pl.multiple_of(t * half + pair * 128, 128), 128)] = values.astype(LOW)
+                gqkv[here, t * half + pair * 128 : t * half + pair * 128 + 128] = values.astype(LOW)
             return inner
 
         lax.fori_loop(0, rows // 64, one, 0)
         return carry
 
-    lax.fori_loop(0, pairs, attend_back, 0)
-
-    q_first = [True, True, False, True]
+    for pair in range(pairs):
+        turn()
+        attend_back(pair, 0)
+
     for t in range(3):
+        turn()
         pq[1 + t] = (
             dot(nrm_t[...], gqkv[:, t * half : (t + 1) * half]).reshape(pq.shape[1:]).astype(LOW)
         )
-        group_q.step1(1 + t, q_first[1 + t])
+        first(12 + t)
+
+    turn()
 
     def back_attn(n, carry):
         big[:, chunk(n)] = dot_nt(gqkv[...], wqkv_v[chunk(n), :])
         return carry
 
     lax.fori_loop(0, chunks_w, back_attn, 0)
+    turn()
 
     def pack_gi(yy, b, here, there):
         sb2[yy, there, :] = big[here, 0:width].astype(LOW)
@@ -807,7 +899,36 @@
         0,
     )
     gain_1 = send(gain_s, gain_x, sem_gain_s.at[0], sem_gain_r.at[0], x_dev)
+    gain_2 = send(gain_x, gain_y, sem_gain_s.at[1], sem_gain_r.at[1], y_dev)
+    gain_3 = [
+        send(gain_y, gain_z.at[d], sem_gain_s.at[2 + d], sem_gain_r.at[2 + d], z_devs[d])
+        for d in range(3)
+    ]
+    gain_4 = send(gain_s, gain_c, sem_gain_s.at[5], sem_gain_r.at[5], sibling)
     gain_1.start()
+
+    def gains_2():
+        gain_1.wait()
+        gain_x[...] = gain_s[...] + gain_x[...]
+        gain_2.start()
+
+    def gains_3():
+        gain_2.wait()
+        gain_y[...] = gain_x[...] + gain_y[...]
+        for copy in gain_3:
+            copy.start()
+
+    def gains_4():
+        for copy in gain_3:
+            copy.wait()
+        gain_s[...] = gain_y[...] + gain_z[0] + gain_z[1] + gain_z[2]
+        gain_4.start()
+
+    def gains_5():
+        gain_4.wait()
+        gain_c[0:8, :] = gain_s[0:8, :] + gain_c[0:8, :]
+        gain_c[...] = pltpu.roll(gain_c[...], lax.rem(8 - i, 8) * (width // 8), 1)
+
     gi_copy.wait_recv()
 
     def finish_gi(yy, b, here, there):
@@ -822,39 +943,15 @@
     gi_across = send(gi.at[1 - y], gi_in, sem_in_s.at[7], sem_in_r.at[7], y_dev)
     gi_across.start()
 
-    todo = []
-    for n in range(chunks_f):
-        todo += [(group_a, n, True), (group_a, n + chunks_f, False)]
-    todo += [(group_d, n, d_first[n]) for n in range(chunks_w)]
-    todo += [(group_q, n, q_first[n]) for n in range(4)]
-    lag = 4
-    names = ["step2", "step3", "step4", "step5", "step6"]
-    for tick in range(len(todo) + lag * (len(names) - 1)):
-        for stage in range(len(names) - 1, -1, -1):
-            at = tick - lag * stage
-            if 0 <= at < len(todo):
-                group, k, first = todo[at]
-                getattr(group, names[stage])(k, first)
-
-    gain_1.wait()
-    gain_s[...] = gain_s[...] + gain_x[...]
-    gain_2 = send(gain_s, gain_y, sem_gain_s.at[1], sem_gain_r.at[1], y_dev)
-    gain_2.start()
-    gain_2.wait()
-    gain_s[...] = gain_s[...] + gain_y[...]
-    gain_3 = [
-        send(gain_s, gain_z.at[d], sem_gain_s.at[2 + d], sem_gain_r.at[2 + d], z_devs[d])
-        for d in range(3)
-    ]
-    for copy in gain_3:
-        copy.start()
-    for copy in gain_3:
-        copy.wait()
-    gain_s[...] = gain_s[...] + gain_z[0] + gain_z[1] + gain_z[2]
-    gain_4 = send(gain_s, gain_c, sem_gain_s.at[5], sem_gain_r.at[5], sibling)
-    gain_4.start()
-    gain_4.wait()
-    gain_c[0:8, :] = gain_s[0:8, :] + gain_c[0:8, :]
+    tail = next(slots)
+    gains_at = dict(zip((4, 10, 16, 22), (gains_2, gains_3, gains_4, gains_5)))
+    for n, code in enumerate(tail):
+        if n in gains_at:
+            gains_at[n]()
+        group, k = chunks[code // 10]
+        getattr(group, f"step{code % 10}")(k)
+    for group, k in chunks:
+        group.end(k)
 
     outs = [
         pltpu.make_async_copy(fa, fa_hbm, sem_o.at[2]),
@@ -885,13 +982,24 @@
         gnf_copy(n).wait_send()
     bo_copy.wait_send()
     gi_copy.wait_send()
-    for group, k, first in todo:
-        group.sent(k, first)
-
-
-def spread(chunks_f, fa, fd, fq, bo, gi, bo_out, gi_out, dq, dk, dv, do, dg, du, dd):
+    for group, k in chunks:
+        group.sent(k)
+
+
+def spread(chunks_f, share, *refs):
+    far, refs = refs[:6], refs[6:]
+    outs, near, sem = refs[:11], refs[11:17], refs[17]
+    bo_out, gi_out, da, dq, dk, dv, do, df, dg, du, dd = outs
+    copies = [pltpu.make_async_copy(a, b, sem.at[n]) for n, (a, b) in enumerate(zip(far, near))]
+    for copy in copies:
+        copy.start()
+    fa, fd, fq, bo, gi, gains = near
+    for copy in copies:
+        copy.wait()
     bo_out[...] = bo[...]
     gi_out[...] = gi[...]
+    da[...] = gains[0, 0:share]
+    df[...] = gains[8, 0:share]
     rows = fa.shape[3]
     for core in range(2):
         for h in range(2):
@@ -932,7 +1040,7 @@
         return [
             pltpu.VMEM((n, 4, 2, 2, r, w), LOW),
             pltpu.VMEM((n, 4, 2, r, w), LOW),
-            pltpu.VMEM((n, 4, r, w), LOW),
+            pltpu.VMEM((n, 6, r, w), LOW),
             pltpu.VMEM((n, 3, r, w), LOW),
             pltpu.VMEM((n, 2, 2, r, w), LOW),
         ]
@@ -982,26 +1090,28 @@
         ),
         name="block",
     )(
-        lengths, gain_attn.reshape(1, width), gain_ffn.reshape(1, width), block_in, cotangent, tables,
+        lengths, gain_attn, gain_ffn, block_in, cotangent, tables,
         w_query, w_key, w_value, w_out, w_gate, w_up, w_down,
     )
     thick = (width // shares, width)
-    bo, gi, dq, dk, dv, do, dg, du, dd = pl.pallas_call(
-        functools.partial(spread, chunks_f),
+    made = (fa, fd, fq, bo, gi, gains)
+    share = width // shares
+    bo, gi, da, dq, dk, dv, do, df, dg, du, dd = pl.pallas_call(
+        functools.partial(spread, chunks_f, share),
         out_shape=(
-            shape(block_in.shape, LOW), shape(block_in.shape, LOW),
+            shape(block_in.shape, LOW), shape(block_in.shape, LOW), shape((share,), F32),
             shape(thick, F32), shape(thick, F32), shape(thick, F32), shape(thick, F32),
+            shape((share,), F32),
             shape((width // shares, hidden_all), F32), shape((width // shares, hidden_all), F32),
             shape((hidden_all // shares, width), F32),
         ),
-        in_specs=[vmem] * 5,
-        out_specs=(vmem,) * 9,
-        compiler_params=pltpu.CompilerParams(vmem_limit_bytes=32 * 2**20),
+        in_specs=[any_] * 6,
+        out_specs=(vmem,) * 11,
+        scratch_shapes=[pltpu.VMEM(a.shape, a.dtype) for a in made] + [dma((6,))],
+        compiler_params=pltpu.CompilerParams(vmem_limit_bytes=60 * 2**20),
         name="spread",
-    )(fa, fd, fq, bo, gi)
-    share = width // shares
-    gains = lax.dynamic_slice(gains, (0, lax.axis_index("items") * share), (16, share))
-    return bo, gi, gains[0], dq, dk, dv, do, gains[8], dg, du, dd
+    )(*made)
+    return bo, gi, da, dq, dk, dv, do, df, dg, du, dd
 
 
 def solution(mesh):

time: 153 us -> 122 us (0.80)
  Pallas kernels: 143 us -> 121 us
  local copies, waits for them, and re-layouts: 9.1 us -> 0 us
    pallas_call x1, Pallas kernels: 140 us -> 117 us  [item_per_chip(): pl.pallas_call(functools.partial(fused, (rows_here, width, hidden_all)),...]
    unnamed x10 -> x0, local copies, waits for them, and re-layouts: 5.25 us -> none
    reshape x2 -> x0, local copies, waits for them, and re-layouts: 2.53 us -> none  [the longest x1 1.27 us: item_per_chip(): gain_attn.reshape(1, width)]
    pallas_call x1, Pallas kernels: 2.16 us -> 3.92 us  [item_per_chip(): pl.pallas_call(functools.partial(spread, chunks_f, share), out_shape=(sha...]
where the time goes in v2:
time: 122 us
  Pallas kernels  121 us (99%)
    pallas_call x1, Pallas kernels, item_per_chip(): pl.pallas_call(functools.partial(fused, (rows_here, width, hidden_all)),...  117 us
    pallas_call x1, Pallas kernels, item_per_chip(): pl.pallas_call(functools.partial(spread, chunks_f, share), out_shape=(sha...  3.92 us

profile of v2, /device:TPU:1, one launch (start us, length us, event | category | flops | bytes accessed | tf_op | source)
XLA Modules:
  0.0 121.6 jit_solution(2627437571199167785)
XLA Ops:
  0.6 116.8 %block.1 = (bf16[2,160,768]{2,1,0:T(8,128)(2,1)}, bf16[2,160,768]{2,1,0:T(8,128)(2,1)}, bf16[8,2,2,48,256]{4,3,2,1,0:T(8,128)(2,1)}, bf16[3,2,2,64,256]{4,3,2,1,...) custom-call(s32[2]{0:T(128)} %refs_0_.1, f32[768]{0:T(1024)} %refs_1_.1, f32[768]{0:T(1024)} %refs_2_.1, ...), custom_call_target="tpu_custom_call" | custom-call | tf_op jit(solution)/shard_map/block/pallas_call | solution.py:1078
  117.5 3.9 %spread.1 = (bf16[2,160,768]{2,1,0:T(8,128)(2,1)}, bf16[2,160,768]{2,1,0:T(8,128)(2,1)}, f32[96]{0:T(128)}, f32[96,768]{1,0:T(8,128)}, f32[96,768]{1,0:T(8,128)}...) custom-call(bf16[8,2,2,48,256]{4,3,2,1,0:T(8,128)(2,1)} %get-tuple-e, ...), custom_call_target="tpu_custom_call" | custom-call | tf_op jit(solution)/shard_map/spread/pallas_call | solution.py:1099

commit v3 on v2

--- a/solution.py
+++ b/solution.py
@@ -280,26 +280,33 @@
 F32 = jnp.float32
 NEVER = -1e30
 
+PLANS = "yxxzxzyyyyxxxyy"
 ORDER = (
-    (2, 42),
-    (12, 52),
     (),
     (),
-    (22, 62),
-    (3,),
     (),
     (),
-    (32, 72),
-    (13, 43, 53, 82, 63),
-    (23,),
-    (92, 112, 33, 73, 44),
-    (54, 102),
-    (83, 4),
-    (64,),
-    (93,),
+    (2, 42),
+    (52, 12, 62),
+    (),
+    (32,),
+    (),
+    (22,),
+    (72,),
+    (3, 43),
+    (),
+    (63, 53, 82, 13),
+    (102, 33, 92, 73),
+    (23, 4, 44, 64),
+    (14,),
+    (),
+    (112,),
+    (45, 54, 103, 15),
+    (74,),
     (
-        14, 24, 34, 122, 45, 55, 113, 103, 74, 132, 84, 94, 133, 142, 65, 123, 143, 104, 114, 134,
-        75, 85, 95, 124, 105, 144, 135, 145,
+        24, 83, 5, 34, 65, 93, 132, 113, 104, 75, 84, 94, 122, 142, 152, 55, 114, 85, 95, 133,
+        123, 143, 25, 134, 6, 35, 66, 105, 124, 76, 153, 144, 135, 115, 154, 86, 96, 145, 125,
+        155, 136, 146,
     ),
 )
 
@@ -349,7 +356,7 @@
         nrm, nrm_t, qkv, chance, mix_own, mix_in, mix, mix_t,
         mid, nf, nf_t, hid, hid_t, gg, gu, big,
         gnf_out, gnf_in, sb, rb, bo, bo_in, gb, gmx, ds_s, gqkv, sb2, rb2, gi, gi_in,
-        gain_s, gain_x, gain_y, gain_z, gain_c,
+        gain_s, gain_x, gain_y, gain_z, gain_f_z, gain_c,
         pa, r1a, r2a, r3a, fa, pd, r1d, r2d, r3d, fd, pq, r1q, r2q, r3q, fq,
         sem_w, sem_in_s, sem_in_r, sem_core_s, sem_core_r, sem_gain_s, sem_gain_r, sem_o,
         sa_s, sa_r, sd_s, sd_r, sq_s, sq_r,
@@ -373,7 +380,9 @@
     sibling = device(y, 1 - c, z, x)
     y_dev = device(1 - y, c, z, x)
     x_dev = device(y, c, z, 1 - x)
-    z_devs = [device(y, c, lax.rem(z + d, 4), x) for d in (1, 2, 3)]
+    z_hi, z_lo = z // 2, z % 2
+    near_z = device(y, c, z + 1 - 2 * z_lo, x)
+    far_z = device(y, c, z + 2 - 4 * z_hi, x)
 
     started = []
 
@@ -409,9 +418,9 @@
         copy.start()
 
     barrier = pltpu.get_barrier_semaphore()
-    for to in [sibling, y_dev, x_dev] + z_devs:
+    for to in (sibling, y_dev, x_dev, near_z, far_z):
         pl.semaphore_signal(barrier, inc=1, device_id=to, device_id_type=MESH)
-    pl.semaphore_wait(barrier, 6)
+    pl.semaphore_wait(barrier, 5)
 
     s_y = (1 - y) * 2 + c
     across_x = send(x_hbm.at[1 - y], x4.at[s], sem_in_s.at[0], sem_in_r.at[0], y_dev)
@@ -561,50 +570,15 @@
         def copy(self, k, n, src, dst, to):
             return send(src, dst, self.s_sem.at[k, n], self.r_sem.at[k, n], to)
 
-        def add(self, k, to, own):
-            self.r1[to] = (self.r1[to].astype(F32) + self.parts[own].astype(F32)).astype(LOW)
-
-    class ByX(Group):
-        def first(self, k):
-            return self.copy(k, 0, self.parts.at[k, :, 1 - x], self.r1.at[k], x_dev)
-
-        def along_z(self, k, d):
-            return self.copy(
-                k, d, self.r1.at[k, lax.rem(z + d, 4)], self.r2.at[k, pl.ds(2 * d - 2, 2)], z_devs[d - 1]
-            )
-
-        def over_y(self, k):
-            return self.copy(k, 4, self.r1.at[k, z], self.r3.at[k, pl.ds(0, 2)], y_dev)
+        def step1(self, k):
+            self.hop(k, 0).start()
 
         def to_core(self, k):
             return self.copy(k, 5, self.fin.at[k, c], self.fin.at[k, c], sibling)
 
-        def step1(self, k):
-            self.first(k).start()
-
-        def step2(self, k):
-            self.first(k).wait_recv()
-            for d in (1, 2, 3, 0):
-                to = lax.rem(z + d, 4)
-                for h in range(2):
-                    self.add(k, (k, to, h), (k, to, x, h))
-                if d:
-                    self.along_z(k, d).start()
-
-        def step3(self, k):
-            for d in (1, 2, 3):
-                self.along_z(k, d).wait_recv()
+        def finish(self, k, own, new):
             for h in range(2):
-                total = self.r1[k, z, h].astype(F32)
-                for d in (1, 2, 3):
-                    total = total + self.r2[k, 2 * d - 2 + h].astype(F32)
-                self.r1[k, z, h] = total.astype(LOW)
-            self.over_y(k).start()
-
-        def step4(self, k):
-            self.over_y(k).wait_recv()
-            for h in range(2):
-                total = self.r1[k, z, h].astype(F32) + self.r3[k, h].astype(F32)
+                total = self.r1[own + (h,)].astype(F32) + self.r3[k, new + h].astype(F32)
                 self.fin[k, c, h] = total.astype(LOW)
             self.to_core(k).start()
 
@@ -612,80 +586,204 @@
             self.to_core(k).wait_recv()
 
         def sent(self, k):
-            self.first(k).wait_send()
-            for d in (1, 2, 3):
-                self.along_z(k, d).wait_send()
-            self.over_y(k).wait_send()
+            for n in range(self.hops):
+                self.hop(k, n).wait_send()
             self.to_core(k).wait_send()
 
-    class ByY(Group):
-        def first(self, k):
-            return self.copy(k, 0, self.parts.at[k, :, :, 1 - y], self.r1.at[k], y_dev)
-
-        def second(self, k):
-            return self.copy(k, 1, self.r1.at[k, :, 1 - x], self.r2.at[k, pl.ds(0, 4)], x_dev)
-
-        def along_z(self, k, d):
-            return self.copy(
-                k, 1 + d, self.r2.at[k, lax.rem(z + d, 4)], self.r3.at[k, d - 1], z_devs[d - 1]
-            )
-
-        def copies_out(self, k, n):
-            at = self.fin.at[k, c, y] if n < 2 else self.fin.at[k, c, 1 - y]
-            return self.copy(k, 5 + n, at, at, y_dev if n == 0 else sibling)
+    def add(ref, at, other, of):
+        ref[at] = (ref[at].astype(F32) + other[of].astype(F32)).astype(LOW)
+
+    class XZY(Group):
+        hops = 4
+
+        def hop(self, k, n):
+            r1, r2, r3 = self.r1, self.r2, self.r3
+            if n == 0:
+                return self.copy(k, n, self.parts.at[k, :, :, 1 - x], r1.at[k], x_dev)
+            if n == 1:
+                return self.copy(k, n, r1.at[k, :, 1 - z_lo], r2.at[k], near_z)
+            if n == 2:
+                return self.copy(k, n, r1.at[k, 1 - z_hi, z_lo], r3.at[k, pl.ds(0, 2)], far_z)
+            return self.copy(k, n, r1.at[k, z_hi, z_lo], r3.at[k, pl.ds(2, 2)], y_dev)
+
+        def step2(self, k):
+            self.hop(k, 0).wait_recv()
+            for lo in (1 - z_lo, z_lo):
+                for hi in range(2):
+                    for h in range(2):
+                        add(self.r1, (k, hi, lo, h), self.parts, (k, hi, lo, x, h))
+                if lo is not z_lo:
+                    self.hop(k, 1).start()
+
+        def step3(self, k):
+            self.hop(k, 1).wait_recv()
+            for hi in (1 - z_hi, z_hi):
+                for h in range(2):
+                    add(self.r1, (k, hi, z_lo, h), self.r2, (k, hi, h))
+                if hi is not z_hi:
+                    self.hop(k, 2).start()
+
+        def step4(self, k):
+            self.hop(k, 2).wait_recv()
+            for h in range(2):
+                add(self.r1, (k, z_hi, z_lo, h), self.r3, (k, h))
+            self.hop(k, 3).start()
+
+        def step5(self, k):
+            self.hop(k, 3).wait_recv()
+            self.finish(k, (k, z_hi, z_lo), 2)
+
+    class ZXY(Group):
+        hops = 4
+
+        def hop(self, k, n):
+            r1, r2, r3 = self.r1, self.r2, self.r3
+            if n == 0:
+                return self.copy(k, n, self.parts.at[k, :, 1 - z_lo], r1.at[k], near_z)
+            if n == 1:
+                return self.copy(k, n, r1.at[k, 1 - z_hi], r2.at[k], far_z)
+            if n == 2:
+                return self.copy(k, n, r1.at[k, z_hi, 1 - x], r3.at[k, pl.ds(0, 2)], x_dev)
+            return self.copy(k, n, r1.at[k, z_hi, x], r3.at[k, pl.ds(2, 2)], y_dev)
+
+        def step2(self, k):
+            self.hop(k, 0).wait_recv()
+            for hi in (1 - z_hi, z_hi):
+                for xx in range(2):
+                    for h in range(2):
+                        add(self.r1, (k, hi, xx, h), self.parts, (k, hi, z_lo, xx, h))
+                if hi is not z_hi:
+                    self.hop(k, 1).start()
+
+        def step3(self, k):
+            self.hop(k, 1).wait_recv()
+            for xx in (1 - x, x):
+                for h in range(2):
+                    add(self.r1, (k, z_hi, xx, h), self.r2, (k, xx, h))
+                if xx is not x:
+                    self.hop(k, 2).start()
+
+        def step4(self, k):
+            self.hop(k, 2).wait_recv()
+            for h in range(2):
+                add(self.r1, (k, z_hi, x, h), self.r3, (k, h))
+            self.hop(k, 3).start()
+
+        def step5(self, k):
+            self.hop(k, 3).wait_recv()
+            self.finish(k, (k, z_hi, x), 2)
+
+    class YXZ(Group):
+        hops = 5
+
+        def hop(self, k, n):
+            r1, r2, r3 = self.r1, self.r2, self.r3
+            if n == 0:
+                return self.copy(k, n, self.parts.at[k, :, :, :, 1 - y], r1.at[k], y_dev)
+            if n == 1:
+                return self.copy(k, n, r1.at[k, :, :, 1 - x], r2.at[k], x_dev)
+            if n == 2:
+                return self.copy(k, n, r2.at[k, :, 1 - z_lo], r3.at[k, pl.ds(0, 2)], near_z)
+            if n == 3:
+                return self.copy(k, n, r2.at[k, 1 - z_hi, z_lo], r3.at[k, 2], far_z)
+            return self.copy(k, n, self.fin.at[k, c, y], self.fin.at[k, c, y], y_dev)
+
+        def beside(self, k, n):
+            at = self.fin.at[k, c, y] if n == 0 else self.fin.at[k, c, 1 - y]
+            return self.copy(k, 5 + n, at, at, sibling)
+
+        def step2(self, k):
+            self.hop(k, 0).wait_recv()
+            for xx in (1 - x, x):
+                for hi in range(2):
+                    for lo in range(2):
+                        add(self.r1, (k, hi, lo, xx), self.parts, (k, hi, lo, xx, y))
+                if xx is not x:
+                    self.hop(k, 1).start()
+
+        def step3(self, k):
+            self.hop(k, 1).wait_recv()
+            for lo in (1 - z_lo, z_lo):
+                for hi in range(2):
+                    add(self.r2, (k, hi, lo), self.r1, (k, hi, lo, x))
+                if lo is not z_lo:
+                    self.hop(k, 2).start()
+
+        def step4(self, k):
+            self.hop(k, 2).wait_recv()
+            for hi in (1 - z_hi, z_hi):
+                add(self.r2, (k, hi, z_lo), self.r3, (k, hi))
+                if hi is not z_hi:
+                    self.hop(k, 3).start()
+
+        def step5(self, k):
+            self.hop(k, 3).wait_recv()
+            total = self.r2[k, z_hi, z_lo].astype(F32) + self.r3[k, 2].astype(F32)
+            self.fin[k, c, y] = total.astype(LOW)
+            self.hop(k, 4).start()
+            self.beside(k, 0).start()
+
+        def step6(self, k):
+            self.hop(k, 4).wait_recv()
+            self.beside(k, 1).start()
+
+        def end(self, k):
+            for n in range(2):
+                self.beside(k, n).wait_recv()
+
+        def sent(self, k):
+            for n in range(self.hops):
+                self.hop(k, n).wait_send()
+            for n in range(2):
+                self.beside(k, n).wait_send()
+
+    class Gains:
+        def hop(self, k, n):
+            src = (gain_s, gain_x, gain_y, gain_z, gain_s)[n]
+            dst = (gain_x, gain_y, gain_z, gain_f_z, gain_c)[n]
+            to = (x_dev, y_dev, near_z, far_z, sibling)[n]
+            return send(src, dst, sem_gain_s.at[n], sem_gain_r.at[n], to)
 
         def step1(self, k):
-            self.first(k).start()
+            self.hop(k, 0).start()
 
         def step2(self, k):
-            self.first(k).wait_recv()
-            for zz in range(4):
-                self.add(k, (k, zz, 1 - x), (k, zz, 1 - x, y))
-            self.second(k).start()
-            for zz in range(4):
-                self.add(k, (k, zz, x), (k, zz, x, y))
+            self.hop(k, 0).wait()
+            gain_x[...] = gain_s[...] + gain_x[...]
+            self.hop(k, 1).start()
 
         def step3(self, k):
-            self.second(k).wait_recv()
-            for d in (1, 2, 3, 0):
-                to = lax.rem(z + d, 4)
-                self.r2[k, to] = (
-                    self.r2[k, to].astype(F32) + self.r1[k, to, x].astype(F32)
-                ).astype(LOW)
-                if d:
-                    self.along_z(k, d).start()
+            self.hop(k, 1).wait()
+            gain_y[...] = gain_x[...] + gain_y[...]
+            self.hop(k, 2).start()
 
         def step4(self, k):
-            total = self.r2[k, z].astype(F32)
-            for d in (1, 2, 3):
-                self.along_z(k, d).wait_recv()
-                total = total + self.r3[k, d - 1].astype(F32)
-            self.fin[k, c, y] = total.astype(LOW)
-            self.copies_out(k, 0).start()
-            self.copies_out(k, 1).start()
+            self.hop(k, 2).wait()
+            gain_z[...] = gain_y[...] + gain_z[...]
+            self.hop(k, 3).start()
 
         def step5(self, k):
-            self.copies_out(k, 0).wait_recv()
-            self.copies_out(k, 2).start()
+            self.hop(k, 3).wait()
+            gain_s[...] = gain_z[...] + gain_f_z[...]
+            self.hop(k, 4).start()
 
         def end(self, k):
-            self.copies_out(k, 1).wait_recv()
-            self.copies_out(k, 2).wait_recv()
+            self.hop(k, 4).wait()
+            top = lax.broadcasted_iota(jnp.int32, gain_s.shape, 0) == 0
+            total = gain_s[...] + jnp.where(top, gain_c[...], 0.0)
+            gain_c[...] = pltpu.roll(total, lax.rem(8 - i, 8) * (width // 8), 1)
 
         def sent(self, k):
-            self.first(k).wait_send()
-            self.second(k).wait_send()
-            for d in (1, 2, 3):
-                self.along_z(k, d).wait_send()
-            for n in range(3):
-                self.copies_out(k, n).wait_send()
+            pass
 
     buffers_a = (pa, r1a, r2a, r3a, fa, sa_s, sa_r)
     buffers_d = (pd, r1d, r2d, r3d, fd, sd_s, sd_r)
     buffers_q = (pq, r1q, r2q, r3q, fq, sq_s, sq_r)
-    chunks = [(ByX(*buffers_a), n) for n in range(4)] + [(ByY(*buffers_a), n + 4) for n in range(4)]
-    chunks += [(plan(*buffers_d), n) for n, plan in enumerate((ByY, ByY, ByY))]
-    chunks += [(plan(*buffers_q), n) for n, plan in enumerate((ByX, ByX, ByY, ByY))]
+    kinds = {"x": XZY, "y": YXZ, "z": ZXY}
+    chunks = [(kinds[kind](*buffers_a), n) for n, kind in enumerate(PLANS[:8])]
+    chunks += [(kinds[kind](*buffers_d), n) for n, kind in enumerate(PLANS[8:11])]
+    chunks += [(kinds[kind](*buffers_q), n) for n, kind in enumerate(PLANS[11:])]
+    chunks += [(Gains(), 0)]
     slots = iter(ORDER)
 
     def first(chunk):
@@ -721,13 +819,15 @@
         lax.fori_loop(0, rows // fine, one, 0, unroll=5)
         shape = pa.shape[1:]
         pa[n] = dot(nf_t[...], gg[:, at]).reshape(shape).astype(LOW)
-        chunks[0][0].step1(n)
+        first(n)
         pa[n + chunks_f] = dot(nf_t[...], gu[:, at]).reshape(shape).astype(LOW)
-        chunks[4][0].step1(n + chunks_f)
+        first(n + chunks_f)
         hid_t[at, :] = hid[:, at].T
         return carry
 
-    lax.fori_loop(0, chunks_f, feed, 0)
+    for n in range(chunks_f):
+        turn()
+        feed(n, 0)
     turn()
 
     def gnf_copy(n):
@@ -891,44 +991,12 @@
         return total + (big[here, 0:width] * (values * scale)).reshape(step // 8, 8, width).sum(0)
 
     total_a = lax.fori_loop(0, rows // step, gain_back, jnp.zeros((8, width), F32))
-    gain_s[...] = jnp.concatenate(
-        [
-            jnp.broadcast_to(jnp.sum(total_a, 0, keepdims=True), (8, width)),
-            jnp.broadcast_to(jnp.sum(total_f, 0, keepdims=True), (8, width)),
-        ],
-        0,
-    )
-    gain_1 = send(gain_s, gain_x, sem_gain_s.at[0], sem_gain_r.at[0], x_dev)
-    gain_2 = send(gain_x, gain_y, sem_gain_s.at[1], sem_gain_r.at[1], y_dev)
-    gain_3 = [
-        send(gain_y, gain_z.at[d], sem_gain_s.at[2 + d], sem_gain_r.at[2 + d], z_devs[d])
-        for d in range(3)
-    ]
-    gain_4 = send(gain_s, gain_c, sem_gain_s.at[5], sem_gain_r.at[5], sibling)
-    gain_1.start()
-
-    def gains_2():
-        gain_1.wait()
-        gain_x[...] = gain_s[...] + gain_x[...]
-        gain_2.start()
-
-    def gains_3():
-        gain_2.wait()
-        gain_y[...] = gain_x[...] + gain_y[...]
-        for copy in gain_3:
-            copy.start()
-
-    def gains_4():
-        for copy in gain_3:
-            copy.wait()
-        gain_s[...] = gain_y[...] + gain_z[0] + gain_z[1] + gain_z[2]
-        gain_4.start()
-
-    def gains_5():
-        gain_4.wait()
-        gain_c[0:8, :] = gain_s[0:8, :] + gain_c[0:8, :]
-        gain_c[...] = pltpu.roll(gain_c[...], lax.rem(8 - i, 8) * (width // 8), 1)
-
+    row = lax.broadcasted_iota(jnp.int32, (8, width), 0)
+    gain_s[...] = jnp.where(
+        row == 0, jnp.sum(total_a, 0, keepdims=True), jnp.sum(total_f, 0, keepdims=True)
+    )
+    first(15)
+    turn()
     gi_copy.wait_recv()
 
     def finish_gi(yy, b, here, there):
@@ -943,13 +1011,7 @@
     gi_across = send(gi.at[1 - y], gi_in, sem_in_s.at[7], sem_in_r.at[7], y_dev)
     gi_across.start()
 
-    tail = next(slots)
-    gains_at = dict(zip((4, 10, 16, 22), (gains_2, gains_3, gains_4, gains_5)))
-    for n, code in enumerate(tail):
-        if n in gains_at:
-            gains_at[n]()
-        group, k = chunks[code // 10]
-        getattr(group, f"step{code % 10}")(k)
+    turn()
     for group, k in chunks:
         group.end(k)
 
@@ -999,7 +1061,7 @@
     bo_out[...] = bo[...]
     gi_out[...] = gi[...]
     da[...] = gains[0, 0:share]
-    df[...] = gains[8, 0:share]
+    df[...] = gains[1, 0:share]
     rows = fa.shape[3]
     for core in range(2):
         for h in range(2):
@@ -1038,10 +1100,10 @@
 
     def group(n, r, w):
         return [
-            pltpu.VMEM((n, 4, 2, 2, r, w), LOW),
-            pltpu.VMEM((n, 4, 2, r, w), LOW),
-            pltpu.VMEM((n, 6, r, w), LOW),
-            pltpu.VMEM((n, 3, r, w), LOW),
+            pltpu.VMEM((n, 2, 2, 2, 2, r, w), LOW),
+            pltpu.VMEM((n, 2, 2, 2, r, w), LOW),
+            pltpu.VMEM((n, 2, 2, r, w), LOW),
+            pltpu.VMEM((n, 4, r, w), LOW),
             pltpu.VMEM((n, 2, 2, r, w), LOW),
         ]
 
@@ -1065,7 +1127,7 @@
         low(rows, width), low(rows, half), low(rows, rows), low(rows, 3 * half),
         low(2, rows_here, width), low(2, rows_here, width),
         low(2, rows_here, width), low(rows_here, width),
-        full(16, width), full(16, width), full(16, width), full(3, 16, width), full(16, width),
+        full(8, width), full(8, width), full(8, width), full(8, width), full(8, width), full(8, width),
     ]
     scratch += group(2 * chunks_f, thin, WIDE) + group(chunks_w, deep, WIDE) + group(4, thin, half)
     scratch += [
@@ -1080,7 +1142,7 @@
         out_shape=(
             shape(block_in.shape, LOW), shape(block_in.shape, LOW),
             shape((2 * chunks_f, 2, 2, thin, WIDE), LOW), shape((chunks_w, 2, 2, deep, WIDE), LOW),
-            shape((4, 2, 2, thin, half), LOW), shape((16, width), F32),
+            shape((4, 2, 2, thin, half), LOW), shape((8, width), F32),
         ),
         in_specs=[pl.BlockSpec(memory_space=pltpu.SMEM), vmem, vmem] + [any_] * 10,
         out_specs=(any_,) * 6,

time: 122 us -> 110 us (0.902)
  Pallas kernels: 121 us -> 109 us
    pallas_call x1, Pallas kernels: 117 us -> 105 us  [item_per_chip(): pl.pallas_call(functools.partial(fused, (rows_here, width, hidden_all)),...]
where the time goes in v3:
time: 110 us; the launch traced here: 109 us
  Pallas kernels  109 us (99%)
    pallas_call x1, Pallas kernels, item_per_chip(): pl.pallas_call(functools.partial(fused, (rows_here, width, hidden_all)),...  105 us
    pallas_call x1, Pallas kernels, item_per_chip(): pl.pallas_call(functools.partial(spread, chunks_f, share), out_shape=(sha...  3.92 us

profile of v3, /device:TPU:1, one launch (start us, length us, event | category | flops | bytes accessed | tf_op | source)
XLA Modules:
  0.0 109.5 jit_solution(12889867528512245425)
XLA Ops:
  0.6 104.7 %block.1 = (bf16[2,160,768]{2,1,0:T(8,128)(2,1)}, bf16[2,160,768]{2,1,0:T(8,128)(2,1)}, bf16[8,2,2,48,256]{4,3,2,1,0:T(8,128)(2,1)}, bf16[3,2,2,64,256]{4,3,2,1,...) custom-call(s32[2]{0:T(128)} %refs_0_.1, f32[768]{0:T(1024)} %refs_1_.1, f32[768]{0:T(1024)} %refs_2_.1, ...), custom_call_target="tpu_custom_call" | custom-call | tf_op jit(solution)/shard_map/block/pallas_call | solution.py:1140
  105.3 3.9 %spread.1 = (bf16[2,160,768]{2,1,0:T(8,128)(2,1)}, bf16[2,160,768]{2,1,0:T(8,128)(2,1)}, f32[96]{0:T(128)}, f32[96,768]{1,0:T(8,128)}, f32[96,768]{1,0:T(8,128)}...) custom-call(bf16[8,2,2,48,256]{4,3,2,1,0:T(8,128)(2,1)} %get-tuple-e, ...), custom_call_target="tpu_custom_call" | custom-call | tf_op jit(solution)/shard_map/spread/pallas_call | solution.py:1161

commit v4 on v3

--- a/solution.py
+++ b/solution.py
@@ -275,38 +275,44 @@
 
 
 MESH = pl.DeviceIdType.MESH
+SHORT = SIDE_S * SIDE_S + 1
 WIDE = 256
 LOW = jnp.bfloat16
 F32 = jnp.float32
 NEVER = -1e30
 
-PLANS = "yxxzxzyyyyxxxyy"
+PLANS = "xzxzyyyxyxxyyxy"
 ORDER = (
     (),
     (),
     (),
     (),
+    (),
     (2, 42),
-    (52, 12, 62),
+    (12,),
+    (52, 22),
+    (),
+    (),
     (),
     (32,),
+    (62, 72),
     (),
-    (22,),
-    (72,),
-    (3, 43),
+    (43, 3),
+    (13,),
+    (53, 82),
+    (23,),
+    (33,),
+    (92,),
+    (73, 44),
     (),
-    (63, 53, 82, 13),
-    (102, 33, 92, 73),
-    (23, 4, 44, 64),
-    (14,),
     (),
-    (112,),
-    (45, 54, 103, 15),
-    (74,),
+    (4,),
+    (54, 102, 24),
+    (112, 63),
     (
-        24, 83, 5, 34, 65, 93, 132, 113, 104, 75, 84, 94, 122, 142, 152, 55, 114, 85, 95, 133,
-        123, 143, 25, 134, 6, 35, 66, 105, 124, 76, 153, 144, 135, 115, 154, 86, 96, 145, 125,
-        155, 136, 146,
+        14, 93, 74, 45, 55, 83, 34, 122, 103, 64, 94, 84, 132, 152, 104, 142, 65, 5, 85, 25, 113,
+        133, 123, 114, 15, 143, 75, 134, 46, 56, 124, 35, 115, 95, 153, 144, 105, 125, 66, 86,
+        154, 145, 135, 116, 126, 155, 146,
     ),
 )
 
@@ -488,22 +494,48 @@
             mix_own.at[pair], mix_in.at[pair], sem_core_s.at[pair], sem_core_r.at[pair], sibling
         )
 
+    tiles = blocks
+    key = lax.broadcasted_iota(jnp.int32, (1, rows), 1)
+    bias = jnp.where(key < length, 0.0, NEVER)
+
+    def stacked(first, second):
+        return jnp.concatenate([first, second], 0)
+
     def attend(pair, carry):
         lanes = pl.ds(pl.multiple_of(pair * 128, 128), 128)
+        parts = []
+        for k0, kb in tiles:
+            query = qkv[0, k0:, lanes]
+            part = dot_nt(stacked(query * masks[0], query * masks[1]), qkv[1, k0 : k0 + kb, lanes])
+            parts.append(part + bias[:, k0 : k0 + kb] if k0 + kb > SHORT else part)
+        for n in range(2):
+            for r0, rb in blocks:
+                scores = []
+                for (k0, kb), part in zip(tiles, parts):
+                    if k0 <= r0:
+                        base = n * (rows - k0) + r0 - k0
+                        here = part[base : base + rb]
+                        if k0 == r0:
+                            row = lax.broadcasted_iota(jnp.int32, here.shape, 0)
+                            col = lax.broadcasted_iota(jnp.int32, here.shape, 1)
+                            here = jnp.where(col <= row, here, NEVER)
+                        scores.append((k0, kb, here))
+                top = functools.reduce(jnp.maximum, [jnp.max(p, -1, keepdims=True) for _, _, p in scores])
+                expo = [(k0, kb, jnp.exp(p - top)) for k0, kb, p in scores]
+                inverse = 1.0 / sum(jnp.sum(p, -1, keepdims=True) for _, _, p in expo)
+                for k0, kb, p in expo:
+                    chance[pair * 2 + n, r0 : r0 + rb, k0 : k0 + kb] = (p * inverse).astype(LOW)
+        outs = []
+        for k0, kb in tiles:
+            at = slice(k0, k0 + kb)
+            low = stacked(chance[pair * 2, k0:, at], chance[pair * 2 + 1, k0:, at])
+            outs.append(dot(low, qkv[2, at, lanes]))
         for r0, rb in blocks:
-            nk = r0 + rb
-            row = r0 + lax.broadcasted_iota(jnp.int32, (rb, nk), 0)
-            col = lax.broadcasted_iota(jnp.int32, (rb, nk), 1)
-            allowed = (col <= row) & (col < length)
             both = []
             for n in range(2):
-                query = qkv[0, r0:nk, lanes] * masks[n]
-                scores = jnp.where(allowed, dot_nt(query, qkv[1, :nk, lanes]), NEVER)
-                expo = jnp.exp(scores - jnp.max(scores, -1, keepdims=True))
-                low = (expo * (1.0 / jnp.sum(expo, -1, keepdims=True))).astype(LOW)
-                chance[pair * 2 + n, r0:nk, :nk] = low
-                both.append(dot(low, qkv[2, :nk, lanes]))
-            mix_own[pair, r0:nk, :] = jnp.where(left_head, both[0], both[1]).astype(LOW)
+                at = [n * (rows - k0) + r0 - k0 for k0, _ in tiles if k0 <= r0]
+                both.append(sum(out[b : b + rb] for b, out in zip(at, outs)))
+            mix_own[pair, r0 : r0 + rb, :] = jnp.where(left_head, both[0], both[1]).astype(LOW)
         mix_copy(pair).start()
         return carry
 
@@ -842,8 +874,9 @@
         gnf_copy(n).start()
         return carry
 
-    lax.fori_loop(0, chunks_w, back_ffn, 0)
-    turn()
+    for n in range(chunks_w):
+        back_ffn(n, 0)
+        turn()
 
     def down(n, carry):
         big[:, chunk(n + chunks_w)] = dot(hid[...], wd_v[:, chunk(n)])
@@ -917,29 +950,49 @@
     first(11)
     gmx[...] = dot_nt(gb[...], wo_v[mine, :]).astype(LOW)
 
-    def attend_back(pair, carry):
+    def query_back(pair):
         lanes = slice(pair * 128, pair * 128 + 128)
-
-        def keep(n, at, off, value):
-            where_ = slice(off * 128, off * 128 + 128)
-            if n:
-                value = jnp.where(left_head, big[at, where_], value)
-            big[at, where_] = value
-
+        grads = []
+        for k0, kb in tiles:
+            grad = gmx[k0:, lanes]
+            grads.append(
+                dot_nt(stacked(grad * masks[0], grad * masks[1]), qkv[2, k0 : k0 + kb, lanes])
+            )
         for n in range(2):
-            head = pair * 2 + n
-            for r0, rb_ in blocks:
-                nk = r0 + rb_
-                grad = gmx[r0:nk, lanes] * masks[n]
-                prob = chance[head, r0:nk, :nk].astype(F32)
-                each = dot_nt(grad, qkv[2, :nk, lanes]) * prob
-                low = (each - prob * jnp.sum(each, -1, keepdims=True)).astype(LOW)
-                ds_s[r0:nk, :nk] = low
-                keep(n, slice(r0, nk), 0, dot(low, qkv[1, :nk, lanes]))
-            for k0, kb in blocks:
-                at = slice(k0, k0 + kb)
-                keep(n, at, 1, dot_tn(ds_s[k0:, at], qkv[0, k0:, lanes]))
-                keep(n, at, 2, dot_tn(chance[head, k0:, at], gmx[k0:, lanes]))
+            for r0, rb in blocks:
+                both = []
+                for (k0, kb), grad in zip(tiles, grads):
+                    if k0 <= r0:
+                        base = n * (rows - k0) + r0 - k0
+                        prob = chance[pair * 2 + n, r0 : r0 + rb, k0 : k0 + kb].astype(F32)
+                        both.append((slice(k0, k0 + kb), prob, grad[base : base + rb] * prob))
+                inner = sum(jnp.sum(each, -1, keepdims=True) for _, _, each in both)
+                for at, prob, each in both:
+                    ds_s[n, r0 : r0 + rb, at] = (each - prob * inner).astype(LOW)
+        outs = []
+        for k0, kb in tiles:
+            at = slice(k0, k0 + kb)
+            outs.append(dot(stacked(ds_s[0, k0:, at], ds_s[1, k0:, at]), qkv[1, at, lanes]))
+        for r0, rb in blocks:
+            both = []
+            for n in range(2):
+                at = [n * (rows - k0) + r0 - k0 for k0, _ in tiles if k0 <= r0]
+                both.append(sum(out[b : b + rb] for b, out in zip(at, outs)))
+            big[r0 : r0 + rb, 0:128] = jnp.where(left_head, both[0], both[1])
+
+    def keys_back(pair):
+        lanes = slice(pair * 128, pair * 128 + 128)
+
+        def beside(first, second):
+            return jnp.concatenate([first, second], 1)
+
+        for k0, kb in tiles:
+            at = slice(k0, k0 + kb)
+            out = dot_tn(beside(ds_s[0, k0:, at], ds_s[1, k0:, at]), qkv[0, k0:, lanes])
+            big[at, 128:256] = jnp.where(left_head, out[:kb], out[kb:])
+            low = beside(chance[pair * 2, k0:, at], chance[pair * 2 + 1, k0:, at])
+            out = dot_tn(low, gmx[k0:, lanes])
+            big[at, 256:384] = jnp.where(left_head, out[:kb], out[kb:])
 
         def one(b, inner):
             here = pl.ds(pl.multiple_of(b * 64, 64), 64)
@@ -954,12 +1007,13 @@
                 gqkv[here, t * half + pair * 128 : t * half + pair * 128 + 128] = values.astype(LOW)
             return inner
 
-        lax.fori_loop(0, rows // 64, one, 0)
-        return carry
+        lax.fori_loop(0, rows // 64, one, 0, unroll=5)
 
     for pair in range(pairs):
         turn()
-        attend_back(pair, 0)
+        query_back(pair)
+        turn()
+        keys_back(pair)
 
     for t in range(3):
         turn()
@@ -1049,37 +1103,52 @@
 
 
 def spread(chunks_f, share, *refs):
-    far, refs = refs[:6], refs[6:]
-    outs, near, sem = refs[:11], refs[11:17], refs[17]
-    bo_out, gi_out, da, dq, dk, dv, do, df, dg, du, dd = outs
-    copies = [pltpu.make_async_copy(a, b, sem.at[n]) for n, (a, b) in enumerate(zip(far, near))]
-    for copy in copies:
+    fa_far, fd_far, fq_far, bo, gi, gains_far = refs[:6]
+    outs, (fa, fd, fq, gains), stage, sem_in, sem_out = refs[6:17], refs[17:21], refs[21:28], *refs[28:]
+    bo_out, gi_out, da, df = outs[0], outs[1], outs[2], outs[7]
+    ends = outs[3:7] + outs[8:]
+    dq, dk, dv, do, dg, du, dd = stage
+    near = [
+        pltpu.make_async_copy(a, b, sem_in.at[n])
+        for n, (a, b) in enumerate(
+            [(fa_far.at[:chunks_f], fa.at[:chunks_f]), (fa_far.at[chunks_f:], fa.at[chunks_f:])]
+            + [(fd_far, fd), (fq_far, fq), (gains_far, gains), (bo, bo_out), (gi, gi_out)]
+        )
+    ]
+    for copy in near:
         copy.start()
-    fa, fd, fq, bo, gi, gains = near
-    for copy in copies:
-        copy.wait()
-    bo_out[...] = bo[...]
-    gi_out[...] = gi[...]
-    da[...] = gains[0, 0:share]
-    df[...] = gains[1, 0:share]
-    rows = fa.shape[3]
-    for core in range(2):
-        for h in range(2):
-            at = slice(h * rows, (h + 1) * rows)
+    done = [pltpu.make_async_copy(a, b, sem_out.at[n]) for n, (a, b) in enumerate(zip(stage, ends))]
+    rows, half, deep = fa.shape[3], fq.shape[4], fd.shape[3]
+    halves = [(core, h, slice(h * rows, (h + 1) * rows)) for core in range(2) for h in range(2)]
+
+    for first, ref, copy in ((0, dg, 0), (chunks_f, du, 1)):
+        near[copy].wait()
+        for core, h, at in halves:
             for n in range(chunks_f):
                 for b in range(WIDE // 128):
                     far = 256 * (n * (WIDE // 128) + b) + 128 * core
-                    near = slice(128 * b, 128 * (b + 1))
-                    dg[at, far : far + 128] = fa[n, core, h, :, near].astype(F32)
-                    du[at, far : far + 128] = fa[n + chunks_f, core, h, :, near].astype(F32)
-            half = fq.shape[4]
-            lanes = slice(core * half, (core + 1) * half)
-            for n, ref in enumerate((do, dq, dk, dv)):
-                ref[at, lanes] = fq[n, core, h].astype(F32)
-            deep = fd.shape[3]
-            at = slice((2 * core + h) * deep, (2 * core + h + 1) * deep)
-            for n in range(fd.shape[0]):
-                dd[at, WIDE * n : WIDE * (n + 1)] = fd[n, core, h].astype(F32)
+                    ref[at, far : far + 128] = fa[
+                        n + first, core, h, :, 128 * b : 128 * (b + 1)
+                    ].astype(F32)
+        done[4 + copy].start()
+    near[2].wait()
+    for core, h, _ in halves:
+        at = slice((2 * core + h) * deep, (2 * core + h + 1) * deep)
+        for n in range(fd.shape[0]):
+            dd[at, WIDE * n : WIDE * (n + 1)] = fd[n, core, h].astype(F32)
+    done[6].start()
+    near[3].wait()
+    for n, (ref, end) in enumerate(((do, 3), (dq, 0), (dk, 1), (dv, 2))):
+        for core, h, at in halves:
+            ref[at, core * half : (core + 1) * half] = fq[n, core, h].astype(F32)
+        done[end].start()
+    near[4].wait()
+    da[...] = gains[0, 0:share]
+    df[...] = gains[1, 0:share]
+    near[5].wait()
+    near[6].wait()
+    for copy in done:
+        copy.wait()
 
 
 def item_per_chip(
@@ -1124,7 +1193,7 @@
         low(chunks_w, rows, WIDE), low(chunks_w, rows, WIDE),
         low(2, rows_here, width), low(2, rows_here, width),
         low(2, rows_here, width), low(rows_here, width),
-        low(rows, width), low(rows, half), low(rows, rows), low(rows, 3 * half),
+        low(rows, width), low(rows, half), low(2, rows, rows), low(rows, 3 * half),
         low(2, rows_here, width), low(2, rows_here, width),
         low(2, rows_here, width), low(rows_here, width),
         full(8, width), full(8, width), full(8, width), full(8, width), full(8, width), full(8, width),
@@ -1168,8 +1237,11 @@
             shape((hidden_all // shares, width), F32),
         ),
         in_specs=[any_] * 6,
-        out_specs=(vmem,) * 11,
-        scratch_shapes=[pltpu.VMEM(a.shape, a.dtype) for a in made] + [dma((6,))],
+        out_specs=(vmem,) * 3 + (any_,) * 4 + (vmem,) + (any_,) * 3,
+        scratch_shapes=[pltpu.VMEM(a.shape, a.dtype) for a in (fa, fd, fq, gains)]
+        + [pltpu.VMEM(thick, F32)] * 4
+        + [pltpu.VMEM((width // shares, hidden_all), F32)] * 2
+        + [pltpu.VMEM((hidden_all // shares, width), F32), dma((7,)), dma((7,))],
         compiler_params=pltpu.CompilerParams(vmem_limit_bytes=60 * 2**20),
         name="spread",
     )(*made)

time: 110 us -> 106 us (0.964)
  Pallas kernels: 109 us -> 105 us
    pallas_call x1, Pallas kernels: 105 us -> 101 us  [item_per_chip(): pl.pallas_call(functools.partial(fused, (rows_here, width, hidden_all)),...]
where the time goes in v4:
time: 106 us; the launch traced here: 105 us
  Pallas kernels  105 us (99%)
    pallas_call x1, Pallas kernels, item_per_chip(): pl.pallas_call(functools.partial(fused, (rows_here, width, hidden_all)),...  101 us
    pallas_call x1, Pallas kernels, item_per_chip(): pl.pallas_call(functools.partial(spread, chunks_f, share), out_shape=(sha...  3.93 us

profile of v4, /device:TPU:1, one launch (start us, length us, event | category | flops | bytes accessed | tf_op | source)
XLA Modules:
  0.0 105.5 jit_solution(13913393309577810902)
XLA Ops:
  0.6 100.7 %block.1 = (bf16[2,160,768]{2,1,0:T(8,128)(2,1)}, bf16[2,160,768]{2,1,0:T(8,128)(2,1)}, bf16[8,2,2,48,256]{4,3,2,1,0:T(8,128)(2,1)}, bf16[3,2,2,64,256]{4,3,2,1,...) custom-call(s32[2]{0:T(128)} %refs_0_.1, f32[768]{0:T(1024)} %refs_1_.1, f32[768]{0:T(1024)} %refs_2_.1, ...), custom_call_target="tpu_custom_call" | custom-call | tf_op jit(solution)/shard_map/block/pallas_call | solution.py:1209
  101.4 3.9 %spread.1 = (bf16[2,160,768]{2,1,0:T(8,128)(2,1)}, bf16[2,160,768]{2,1,0:T(8,128)(2,1)}, f32[96]{0:T(128)}, f32[96,768]{1,0:T(8,128)}, f32[96,768]{1,0:T(8,128)}...) custom-call(bf16[8,2,2,48,256]{4,3,2,1,0:T(8,128)(2,1)} %get-tuple-e, ...), custom_call_target="tpu_custom_call" | custom-call | tf_op jit(solution)/shard_map/spread/pallas_call | solution.py:1230

commit v5 on v4

--- a/solution.py
+++ b/solution.py
@@ -281,7 +281,7 @@
 F32 = jnp.float32
 NEVER = -1e30
 
-PLANS = "xzxzyyyxyxxyyxy"
+PLANS = "xyzyzxyyzxxyyxy"
 ORDER = (
     (),
     (),
@@ -290,29 +290,29 @@
     (),
     (2, 42),
     (12,),
+    (),
     (52, 22),
+    (62,),
+    (),
+    (13,),
+    (3,),
+    (43,),
+    (32,),
+    (63, 53),
+    (72,),
+    (23,),
+    (92,),
     (),
     (),
     (),
-    (32,),
-    (62, 72),
+    (82,),
     (),
-    (43, 3),
-    (13,),
-    (53, 82),
-    (23,),
-    (33,),
-    (92,),
-    (73, 44),
+    (14, 102, 4, 44, 64, 33, 112, 54),
     (),
-    (),
-    (4,),
-    (54, 102, 24),
-    (112, 63),
     (
-        14, 93, 74, 45, 55, 83, 34, 122, 103, 64, 94, 84, 132, 152, 104, 142, 65, 5, 85, 25, 113,
-        133, 123, 114, 15, 143, 75, 134, 46, 56, 124, 35, 115, 95, 153, 144, 105, 125, 66, 86,
-        154, 145, 135, 116, 126, 155, 146,
+        73, 24, 93, 122, 83, 15, 132, 103, 65, 34, 74, 113, 142, 152, 5, 45, 94, 55, 123, 84, 133,
+        104, 35, 75, 143, 114, 25, 16, 66, 124, 153, 95, 134, 85, 144, 105, 115, 36, 76, 125, 154,
+        135, 145, 116, 126, 155, 146,
     ),
 )
 

time: 106 us -> 103 us (0.972)
  Pallas kernels: 105 us -> 102 us
    pallas_call x1, Pallas kernels: 101 us -> 97.7 us  [item_per_chip(): pl.pallas_call(functools.partial(fused, (rows_here, width, hidden_all)),...]
where the time goes in v5:
time: 103 us
  Pallas kernels  102 us (99%)
    pallas_call x1, Pallas kernels, item_per_chip(): pl.pallas_call(functools.partial(fused, (rows_here, width, hidden_all)),...  97.7 us
    pallas_call x1, Pallas kernels, item_per_chip(): pl.pallas_call(functools.partial(spread, chunks_f, share), out_shape=(sha...  3.93 us

profile of v5, /device:TPU:1, one launch (start us, length us, event | category | flops | bytes accessed | tf_op | source)
XLA Modules:
  0.0 102.5 jit_solution(9919812542262721007)
XLA Ops:
  0.6 97.7 %block.1 = (bf16[2,160,768]{2,1,0:T(8,128)(2,1)}, bf16[2,160,768]{2,1,0:T(8,128)(2,1)}, bf16[8,2,2,48,256]{4,3,2,1,0:T(8,128)(2,1)}, bf16[3,2,2,64,256]{4,3,2,1,...) custom-call(s32[2]{0:T(128)} %refs_0_.1, f32[768]{0:T(1024)} %refs_1_.1, f32[768]{0:T(1024)} %refs_2_.1, ...), custom_call_target="tpu_custom_call" | custom-call | tf_op jit(solution)/shard_map/block/pallas_call | solution.py:1209
  98.4 3.9 %spread.1 = (bf16[2,160,768]{2,1,0:T(8,128)(2,1)}, bf16[2,160,768]{2,1,0:T(8,128)(2,1)}, f32[96]{0:T(128)}, f32[96,768]{1,0:T(8,128)}, f32[96,768]{1,0:T(8,128)}...) custom-call(bf16[8,2,2,48,256]{4,3,2,1,0:T(8,128)(2,1)} %get-tuple-e, ...), custom_call_target="tpu_custom_call" | custom-call | tf_op jit(solution)/shard_map/spread/pallas_call | solution.py:1230

commit v6 on v5

--- a/solution.py
+++ b/solution.py
@@ -1065,28 +1065,27 @@
     gi_across = send(gi.at[1 - y], gi_in, sem_in_s.at[7], sem_in_r.at[7], y_dev)
     gi_across.start()
 
-    turn()
-    for group, k in chunks:
-        group.end(k)
-
     outs = [
+        pltpu.make_async_copy(bo.at[y], bo_hbm.at[y], sem_o.at[6]),
+        pltpu.make_async_copy(gi.at[y], gi_hbm.at[y], sem_o.at[7]),
+        pltpu.make_async_copy(bo_in, bo_hbm.at[1 - y], sem_o.at[8]),
+        pltpu.make_async_copy(gi_in, gi_hbm.at[1 - y], sem_o.at[9]),
         pltpu.make_async_copy(fa, fa_hbm, sem_o.at[2]),
         pltpu.make_async_copy(fd, fd_hbm, sem_o.at[3]),
         pltpu.make_async_copy(fq, fq_hbm, sem_o.at[4]),
         pltpu.make_async_copy(gain_c, gain_hbm, sem_o.at[5]),
-        pltpu.make_async_copy(bo.at[y], bo_hbm.at[y], sem_o.at[6]),
-        pltpu.make_async_copy(gi.at[y], gi_hbm.at[y], sem_o.at[7]),
     ]
-    for copy in outs:
-        copy.start()
+    outs[0].start()
+    outs[1].start()
+    turn()
     bo_across.wait_recv()
+    outs[2].start()
     gi_across.wait_recv()
-    outs += [
-        pltpu.make_async_copy(bo_in, bo_hbm.at[1 - y], sem_o.at[8]),
-        pltpu.make_async_copy(gi_in, gi_hbm.at[1 - y], sem_o.at[9]),
-    ]
-    for copy in outs[6:]:
-        copy.start()
+    outs[3].start()
+    for n, part in enumerate((chunks[:8], chunks[8:11], chunks[11:15], chunks[15:])):
+        for group, k in part:
+            group.end(k)
+        outs[4 + n].start()
     for copy in outs:
         copy.wait()
 

time: 103 us -> 102 us (level)
  no operation moved by 1% of the time
where the time goes in v6:
time: 102 us
  Pallas kernels  101 us (99%)
    pallas_call x1, Pallas kernels, item_per_chip(): pl.pallas_call(functools.partial(fused, (rows_here, width, hidden_all)),...  97 us
    pallas_call x1, Pallas kernels, item_per_chip(): pl.pallas_call(functools.partial(spread, chunks_f, share), out_shape=(sha...  3.93 us

profile of v6, /device:TPU:1, one launch (start us, length us, event | category | flops | bytes accessed | tf_op | source)
XLA Modules:
  0.0 101.8 jit_solution(720768690488634030)
XLA Ops:
  0.6 97.0 %block.1 = (bf16[2,160,768]{2,1,0:T(8,128)(2,1)}, bf16[2,160,768]{2,1,0:T(8,128)(2,1)}, bf16[8,2,2,48,256]{4,3,2,1,0:T(8,128)(2,1)}, bf16[3,2,2,64,256]{4,3,2,1,...) custom-call(s32[2]{0:T(128)} %refs_0_.1, f32[768]{0:T(1024)} %refs_1_.1, f32[768]{0:T(1024)} %refs_2_.1, ...), custom_call_target="tpu_custom_call" | custom-call | tf_op jit(solution)/shard_map/block/pallas_call | solution.py:1208
  97.7 3.9 %spread.1 = (bf16[2,160,768]{2,1,0:T(8,128)(2,1)}, bf16[2,160,768]{2,1,0:T(8,128)(2,1)}, f32[96]{0:T(128)}, f32[96,768]{1,0:T(8,128)}, f32[96,768]{1,0:T(8,128)}...) custom-call(bf16[8,2,2,48,256]{4,3,2,1,0:T(8,128)(2,1)} %get-tuple-e, ...), custom_call_target="tpu_custom_call" | custom-call | tf_op jit(solution)/shard_map/spread/pallas_call | solution.py:1229

commit v7 on v6

--- a/solution.py
+++ b/solution.py
@@ -429,30 +429,40 @@
     pl.semaphore_wait(barrier, 5)
 
     s_y = (1 - y) * 2 + c
-    across_x = send(x_hbm.at[1 - y], x4.at[s], sem_in_s.at[0], sem_in_r.at[0], y_dev)
+    part_rows = rows_here // 2
+    across_x = [
+        send(
+            x_hbm.at[1 - y, pl.ds(n * part_rows, part_rows)], x4.at[s, pl.ds(n * part_rows, part_rows)],
+            sem_in_s.at[8 + n], sem_in_r.at[8 + n], y_dev,
+        )
+        for n in range(2)
+    ]
     beside_x = send(x_hbm.at[y], x4.at[s], sem_in_s.at[1], sem_in_r.at[1], sibling)
-    across_x.start()
+    for copy in across_x:
+        copy.start()
     beside_x.start()
     across_c = send(cot_hbm.at[1 - y], cot4.at[s], sem_in_s.at[2], sem_in_r.at[2], y_dev)
     beside_c = send(cot_hbm.at[y], cot4.at[s], sem_in_s.at[3], sem_in_r.at[3], sibling)
     own_cot.start()
     for copy in weights[4:]:
         copy.start()
-    relay_x = send(x4.at[s_y], x4.at[s_y], sem_in_s.at[4], sem_in_r.at[4], sibling)
+    relay_x = [
+        send(
+            x4.at[s_y, pl.ds(n * part_rows, part_rows)], x4.at[s_y, pl.ds(n * part_rows, part_rows)],
+            sem_in_s.at[10 + n], sem_in_r.at[10 + n], sibling,
+        )
+        for n in range(2)
+    ]
     relay_c = send(cot4.at[s_y], cot4.at[s_y], sem_in_s.at[5], sem_in_r.at[5], sibling)
 
     length = lens[y]
 
-    def norm_rows(piece):
-        def one(b, carry):
-            here = pl.ds(pl.multiple_of(b * step, step), step)
-            values = x4[piece, here, :].astype(F32)
-            scale = lax.rsqrt(jnp.mean(values * values, -1, keepdims=True) + epsilon)
-            there = pl.ds(pl.multiple_of(piece * rows_here + b * step, step), step)
-            nrm[there, :] = (values * scale * gain_a[...]).astype(LOW)
-            return carry
-
-        lax.fori_loop(0, per, one, 0)
+    def norm_rows(piece, n):
+        here = pl.ds(n * part_rows, part_rows)
+        values = x4[piece, here, :].astype(F32)
+        scale = lax.rsqrt(jnp.mean(values * values, -1, keepdims=True) + epsilon)
+        there = pl.ds(pl.multiple_of(piece * rows_here + n * part_rows, 16), part_rows)
+        nrm[there, :] = (values * scale * gain_a[...]).astype(LOW)
 
     def project_rows(part):
         base = pl.multiple_of(part * 2 * rows_here, 32)
@@ -470,19 +480,23 @@
                 qkv[t, here, 128 * p : 128 * (p + 1)] = lanes.astype(LOW)
 
     own_x.wait()
-    norm_rows(s)
+    for n in range(2):
+        norm_rows(s, n)
     beside_x.wait_recv()
-    norm_rows(2 * y + 1 - c)
+    for n in range(2):
+        norm_rows(2 * y + 1 - c, n)
     for copy in weights[:4]:
         copy.wait()
     project_rows(y)
-    across_x.wait_recv()
-    relay_x.start()
+    for n in range(2):
+        across_x[n].wait_recv()
+        relay_x[n].start()
+        norm_rows(s_y, n)
     across_c.start()
     beside_c.start()
-    norm_rows(s_y)
-    relay_x.wait_recv()
-    norm_rows(2 * (1 - y) + 1 - c)
+    for n in range(2):
+        relay_x[n].wait_recv()
+        norm_rows(2 * (1 - y) + 1 - c, n)
     project_rows(1 - y)
 
     lane = lax.broadcasted_iota(jnp.int32, (1, 128), 1)
@@ -561,23 +575,24 @@
 
     place_mix(mix_own, c)
     turn_rows(nrm, nrm_t)
+    weights[4].wait()
+
+    def chunk(n, wide=WIDE):
+        return pl.ds(pl.multiple_of(n * wide, wide), wide)
+
+    def heads_of_core(core):
+        return pl.ds(pl.multiple_of(core * half, half), half)
+
+    for n in range(width // WIDE):
+        mid[:, chunk(n)] = (
+            dot(mix[:, heads_of_core(c)], wo_v[heads_of_core(c), chunk(n)])
+            + x4[:, :, chunk(n)].reshape(rows, WIDE).astype(F32)
+        )
     for p in range(pairs):
         mix_copy(p).wait_recv()
     place_mix(mix_in, 1 - c)
-
-    weights[4].wait()
-
-    def chunk(n, wide=WIDE):
-        return pl.ds(pl.multiple_of(n * wide, wide), wide)
-
-    def out_project(n, carry):
-        mid[:, chunk(n)] = (
-            dot(mix[...], wo_v[:, chunk(n)])
-            + x4[:, :, chunk(n)].reshape(rows, WIDE).astype(F32)
-        )
-        return carry
-
-    lax.fori_loop(0, width // WIDE, out_project, 0)
+    for n in range(width // WIDE):
+        mid[:, chunk(n)] += dot(mix[:, heads_of_core(1 - c)], wo_v[heads_of_core(1 - c), chunk(n)])
 
     def second_norm(b, carry):
         here = pl.ds(pl.multiple_of(b * step, step), step)
@@ -1089,7 +1104,7 @@
     for copy in outs:
         copy.wait()
 
-    for copy in (across_x, beside_x, across_c, beside_c, relay_x, relay_c, bo_across, gi_across):
+    for copy in (*across_x, beside_x, across_c, beside_c, *relay_x, relay_c, bo_across, gi_across):
         copy.wait_send()
     for p in range(pairs):
         mix_copy(p).wait_send()
@@ -1199,7 +1214,7 @@
     ]
     scratch += group(2 * chunks_f, thin, WIDE) + group(chunks_w, deep, WIDE) + group(4, thin, half)
     scratch += [
-        dma((5 + 3 * (ff // 128),)), dma((8,)), dma((8,)),
+        dma((5 + 3 * (ff // 128),)), dma((12,)), dma((12,)),
         dma((pairs + chunks_w + 2,)), dma((pairs + chunks_w + 2,)), dma((6,)), dma((6,)), dma((10,)),
         dma((2 * chunks_f, 8)), dma((2 * chunks_f, 8)), dma((chunks_w, 8)), dma((chunks_w, 8)),
         dma((4, 8)), dma((4, 8)),

time: 102 us -> 102 us (level)
  no operation moved by 1% of the time
where the time goes in v7:
time: 102 us; the launch traced here: 101 us
  Pallas kernels  101 us (99%)
    pallas_call x1, Pallas kernels, item_per_chip(): pl.pallas_call(functools.partial(fused, (rows_here, width, hidden_all)),...  96.6 us
    pallas_call x1, Pallas kernels, item_per_chip(): pl.pallas_call(functools.partial(spread, chunks_f, share), out_shape=(sha...  3.93 us

profile of v7, /device:TPU:1, one launch (start us, length us, event | category | flops | bytes accessed | tf_op | source)
XLA Modules:
  0.0 101.4 jit_solution(15696611295593714527)
XLA Ops:
  0.6 96.6 %block.1 = (bf16[2,160,768]{2,1,0:T(8,128)(2,1)}, bf16[2,160,768]{2,1,0:T(8,128)(2,1)}, bf16[8,2,2,48,256]{4,3,2,1,0:T(8,128)(2,1)}, bf16[3,2,2,64,256]{4,3,2,1,...) custom-call(s32[2]{0:T(128)} %refs_0_.1, f32[768]{0:T(1024)} %refs_1_.1, f32[768]{0:T(1024)} %refs_2_.1, ...), custom_call_target="tpu_custom_call" | custom-call | tf_op jit(solution)/shard_map/block/pallas_call | solution.py:1223
  97.3 3.9 %spread.1 = (bf16[2,160,768]{2,1,0:T(8,128)(2,1)}, bf16[2,160,768]{2,1,0:T(8,128)(2,1)}, f32[96]{0:T(128)}, f32[96,768]{1,0:T(8,128)}, f32[96,768]{1,0:T(8,128)}...) custom-call(bf16[8,2,2,48,256]{4,3,2,1,0:T(8,128)(2,1)} %get-tuple-e, ...), custom_call_target="tpu_custom_call" | custom-call | tf_op jit(solution)/shard_map/spread/pallas_call | solution.py:1244
